TPU v7x, 256 devices: a whole 4x4x8 slice. The times are simulated.
256 devices in a mesh: dp: 64 (over x, z, core), tensor: 4 (over y).
Axes of the slice: x: 4, y: 4, z: 8, core: 2. Of those that a mesh axis runs over, the one named last changes fastest.
Arguments:
- patches: bfloat16 [24576, 1408], P('dp', 'tensor'), may hold values from -6 to 6
- seg_ids: int32 [16384], P('dp'), may hold values from 0 to 16383, as said below
- cut: int32 [64, 2], P('dp'), may hold values from -64 to 64, as said below
- w_qkv: bfloat16 [3, 704, 1408], P(None, 'tensor'), may hold values from -0.15625 to 0.15625
- w_out: bfloat16 [704, 1408], P('tensor'), may hold values from -0.21875 to 0.21875
- grad_out: bfloat16 [16384, 1408], P('dp', 'tensor'), may hold values from -6 to 6
Outputs:
- mixed: bfloat16 [16384, 1408], P('dp', 'tensor')
- grad_patches: bfloat16 [24576, 1408], P('dp', 'tensor')
- grad_w_qkv: float32 [3, 704, 1408], P(None, 'tensor', 'dp')
- grad_w_out: float32 [704, 1408], P('tensor', 'dp')
Inputs may be any that keep to these rules, and one draw needn't show every extreme that they name: Source block i holds, from its row 0 and in order, the packed rows 256 i + cut[i,0] up to 256 (i + 1) + cut[i,1] - 1. cut[i,1] equals cut[i+1,0]; the first block's cut[.,0] and the last block's cut[.,1] are 0. In every draw one sequence takes 64 rows from each of its two neighbouring blocks. seg_ids[r] is the packed index of the first row of r's image; an image lies within one sequence and within one source block, and seg_ids never falls. The last packed row is an image of its own.
All inputs are finite; a program needn't handle non-finite values.
Results may differ from a plain program's by a relative error of at most 0.0093.
Values may be sent and summed in bfloat16 or wider, within the bound.
A program may use at most 64 MiB of HBM per device.

v0:
```python
import math

import jax
import jax.numpy as jnp
from jax import lax
from jax.sharding import PartitionSpec as P

HD = 88


norm_eps = 1e-06


def from_behind(block, axis, distance):
    devices = range(lax.axis_size(axis))
    route = [(i - distance, i) for i in devices if i - distance in devices]
    return lax.ppermute(block, axis, route)


def row_norm(values):
    center = values - jnp.mean(values, axis=-1, keepdims=True)
    spread = jnp.mean(center * center, axis=-1, keepdims=True)
    inverse = lax.rsqrt(spread + norm_eps)
    return (center * inverse, inverse)


def norm_back(upstream, normed, inverse):
    first_mean = jnp.mean(upstream, axis=-1, keepdims=True)
    second_mean = jnp.mean(upstream * normed, axis=-1, keepdims=True)
    return inverse * (upstream - first_mean - normed * second_mean)


def window(source_array, offset, length):
    filler = jnp.zeros((length,) + source_array.shape[1:], source_array.dtype)
    padded = jnp.concatenate([filler, source_array, filler], axis=0)
    return lax.dynamic_slice_in_dim(padded, length + offset, length, 0)


def expand(condition, member):
    return condition.reshape(condition.shape + (1,) * (member.ndim - 1))


def packing_sends(member, lower_cut, upper_cut, seq_rows):
    spill_rows = (member.shape[0] - seq_rows) // 2
    block_length = seq_rows + upper_cut - lower_cut
    ahead = jnp.maximum(upper_cut, 0)
    return (window(member, block_length - ahead, spill_rows), window(member, 0, spill_rows))


def packing_assemble(member, from_prev, from_next, lower_cut, upper_cut, seq_rows):
    head_rows = jnp.maximum(lower_cut, 0)
    tail_rows = jnp.maximum(-upper_cut, 0)
    position = lax.broadcasted_iota(jnp.int32, (seq_rows,), 0)
    own_rows = window(member, -lower_cut, seq_rows)
    early_rows = window(from_prev, 0, seq_rows)
    late_rows = window(from_next, tail_rows - seq_rows, seq_rows)
    use_early = expand(position < head_rows, own_rows)
    use_late = expand(position >= seq_rows - tail_rows, own_rows)
    return jnp.where(use_early, early_rows, jnp.where(use_late, late_rows, own_rows))


def return_sends(member, upper_cut, spill_rows):
    seq_rows = member.shape[0]
    tail_rows = jnp.maximum(-upper_cut, 0)
    return (window(member, seq_rows - tail_rows, spill_rows), window(member, 0, spill_rows))


def return_assemble(member, from_prev, from_next, lower_cut, upper_cut, src_rows, fill_value):
    seq_rows = member.shape[0]
    block_length = seq_rows + upper_cut - lower_cut
    behind = jnp.maximum(-lower_cut, 0)
    ahead = jnp.maximum(upper_cut, 0)
    position = lax.broadcasted_iota(jnp.int32, (src_rows,), 0)
    own_rows = window(member, lower_cut, src_rows)
    early_rows = window(from_prev, 0, src_rows)
    late_rows = window(from_next, ahead - block_length, src_rows)
    use_early = expand(position < behind, own_rows)
    use_late = expand((position >= block_length - ahead) & (position < block_length), own_rows)
    merged = jnp.where(use_early, early_rows, jnp.where(use_late, late_rows, own_rows))
    return jnp.where(expand(position < block_length, own_rows), merged, fill_value)


def image_weights(query_block, query_ids, key_rows, key_ids, score_scale):
    scores = (
        jnp.einsum("qhe,khe->hqk", query_block, key_rows, preferred_element_type=jnp.float32)
        * score_scale
    )
    same_image = (query_ids[:, None] == key_ids[None, :])[None]
    raised = jnp.where(same_image, jnp.exp(scores), 0.0)
    return raised / jnp.sum(raised, axis=-1, keepdims=True)


def attend_forward(queries, key_rows, values, image_ids, block_rows, score_scale):
    block_count = queries.shape[0] // block_rows

    def one_block(block_args):
        query_block, query_ids = block_args
        weights = image_weights(query_block, query_ids, key_rows, image_ids, score_scale)
        weights_low = weights.astype(jnp.bfloat16)
        return jnp.einsum(
            "hqk,khe->qhe", weights_low, values, preferred_element_type=jnp.float32
        ).astype(jnp.bfloat16)

    block_queries = queries.reshape((block_count, block_rows) + queries.shape[1:])
    outputs = lax.map(one_block, (block_queries, image_ids.reshape(block_count, block_rows)))
    return outputs.reshape(queries.shape)


def attend_backward(queries, key_rows, values, image_ids, grad_att, block_rows, score_scale):
    block_count = queries.shape[0] // block_rows

    def one_block(totals, block_args):
        key_total, value_total = totals
        query_block, query_ids, grad_block = block_args
        weights = image_weights(query_block, query_ids, key_rows, image_ids, score_scale)
        weights_low = weights.astype(jnp.bfloat16)
        grad_weights = jnp.einsum(
            "qhe,khe->hqk", grad_block, values, preferred_element_type=jnp.float32
        )
        inner_sum = jnp.sum(grad_weights * weights, axis=-1, keepdims=True)
        grad_scores = (weights * (grad_weights - inner_sum) * score_scale).astype(jnp.bfloat16)
        grad_query = jnp.einsum(
            "hqk,khe->qhe", grad_scores, key_rows, preferred_element_type=jnp.float32
        )
        key_total = key_total + jnp.einsum(
            "hqk,qhe->khe", grad_scores, query_block, preferred_element_type=jnp.float32
        )
        value_total = value_total + jnp.einsum(
            "hqk,qhe->khe", weights_low, grad_block, preferred_element_type=jnp.float32
        )
        return ((key_total, value_total), grad_query)

    empty = jnp.zeros(key_rows.shape, jnp.float32)
    block_shape = (block_count, block_rows) + queries.shape[1:]
    sweep_args = (
        queries.reshape(block_shape),
        image_ids.reshape(block_count, block_rows),
        grad_att.reshape(block_shape),
    )
    (grad_key, grad_value), grad_query = lax.scan(one_block, (empty, empty), sweep_args)
    return (grad_query.reshape(queries.shape), grad_key, grad_value)


def layer_pass(columns, image_ids, grad_columns, w_qkv, w_out):
    full_rows = lax.all_gather(columns, "tensor", axis=1, tiled=True)
    row_count, model_width = full_rows.shape
    normed, inverse = row_norm(full_rows.astype(jnp.float32))
    normed_low = normed.astype(jnp.bfloat16)
    qkv_flat = w_qkv.reshape(-1, model_width)
    projected = jnp.einsum(
        "rd,cd->rc", normed_low, qkv_flat, preferred_element_type=jnp.float32
    ).reshape(row_count, 3, -1, HD)
    query_hat, query_inverse = row_norm(projected[:, 0])
    key_hat, key_inverse = row_norm(projected[:, 1])
    queries = query_hat.astype(jnp.bfloat16)
    key_rows = key_hat.astype(jnp.bfloat16)
    values = projected[:, 2].astype(jnp.bfloat16)
    score_scale = HD ** (-0.5)
    attended = attend_forward(queries, key_rows, values, image_ids, row_count, score_scale).reshape(
        row_count, -1
    )
    partial_value = jnp.dot(attended, w_out, preferred_element_type=jnp.float32)
    branch = lax.psum_scatter(
        partial_value.astype(jnp.bfloat16), "tensor", scatter_dimension=1, tiled=True
    ).astype(jnp.float32)
    mixed_cols = (columns.astype(jnp.float32) + branch).astype(jnp.bfloat16)
    grad_full = lax.all_gather(grad_columns, "tensor", axis=1, tiled=True)
    grad_att = jnp.einsum("rd,qd->rq", grad_full, w_out, preferred_element_type=jnp.float32).astype(
        jnp.bfloat16
    )
    out_grad_part = jnp.einsum("rq,rd->qd", attended, grad_full, preferred_element_type=jnp.float32)
    grad_query, grad_key, grad_value = attend_backward(
        queries,
        key_rows,
        values,
        image_ids,
        grad_att.reshape(row_count, -1, HD),
        row_count,
        score_scale,
    )
    grad_proj = jnp.stack(
        [
            norm_back(grad_query, query_hat, query_inverse),
            norm_back(grad_key, key_hat, key_inverse),
            grad_value,
        ],
        axis=1,
    )
    grad_proj = grad_proj.astype(jnp.bfloat16).reshape(row_count, -1)
    qkv_grad_part = jnp.einsum(
        "rc,rd->cd", grad_proj, normed_low, preferred_element_type=jnp.float32
    ).reshape(w_qkv.shape)
    input_part = jnp.einsum("rc,cd->rd", grad_proj, qkv_flat, preferred_element_type=jnp.float32)
    share_cols = model_width // lax.axis_size("tensor")
    col_start = lax.axis_index("tensor") * share_cols
    summed = lax.psum(input_part.astype(jnp.bfloat16), "tensor").astype(jnp.float32)
    back_cols = lax.dynamic_slice_in_dim(
        norm_back(summed, normed, inverse), col_start, share_cols, 1
    )
    grad_x_cols = (grad_columns.astype(jnp.float32) + back_cols).astype(jnp.bfloat16)
    return (mixed_cols, grad_x_cols, qkv_grad_part, out_grad_part)


def body(patches, seg_ids, cut, w_qkv, w_out, grad_out):
    seq_rows = seg_ids.shape[0]
    src_rows = patches.shape[0]
    spill_rows = (src_rows - seq_rows) // 2
    lower_cut = cut[0, 0]
    upper_cut = cut[0, 1]
    send_next, send_prev = packing_sends(patches, lower_cut, upper_cut, seq_rows)
    from_prev = from_behind(send_next, "dp", 1)
    from_next = from_behind(send_prev, "dp", -1)
    columns = packing_assemble(patches, from_prev, from_next, lower_cut, upper_cut, seq_rows)
    mixed_cols, grad_x_cols, qkv_grad_part, out_grad_part = layer_pass(
        columns, seg_ids, grad_out, w_qkv, w_out
    )
    back_next, back_prev = return_sends(grad_x_cols, upper_cut, spill_rows)
    back_from_prev = from_behind(back_next, "dp", 1)
    back_from_next = from_behind(back_prev, "dp", -1)
    grad_patches = return_assemble(
        grad_x_cols, back_from_prev, back_from_next, lower_cut, upper_cut, src_rows, 0
    )
    qkv_grad, out_grad = (
        lax.psum_scatter(qkv_grad_part, "dp", scatter_dimension=2, tiled=True),
        lax.psum_scatter(out_grad_part, "dp", scatter_dimension=1, tiled=True),
    )
    total_scale = 1.0 / math.sqrt(seq_rows * lax.axis_size("dp"))
    return (mixed_cols, grad_patches, qkv_grad * total_scale, out_grad * total_scale)


def solution(mesh):
    in_specs = (
        P("dp", "tensor"),
        P("dp"),
        P("dp", None),
        P(None, "tensor", None),
        P("tensor", None),
        P("dp", "tensor"),
    )
    out_specs = (P("dp", "tensor"), P("dp", "tensor"), P(None, "tensor", "dp"), P("tensor", "dp"))
    return jax.shard_map(body, mesh=mesh, in_specs=in_specs, out_specs=out_specs, check_vma=False)
```

profile of v0, /device:TPU:1, one launch (start us, length us, event | category | flops | bytes accessed | tf_op | source)
XLA Modules:
  0.0 432.8 jit_solution(14712648288971283233)
XLA Ops:
  7.2 1.4 fusion.68
  10.6 1.2 fusion.65
  11.8 5.1 %collective-permute-start.1 = (bf16[64,352]{0,1:T(8,128)(2,1)S(1)}, bf16[64,352]{0,1:T(8,128)(2,1)S(1)}, u32[]{:S(2)}, u32[]{:S(2)}) collective-permute-start(bf16[64,352]{0,1:T(8,128)(2,1)S(1)} %get-tuple-element.70), channel_id=1, source_target_pairs={{4,0},{8,4},{12,8},{16,12},{20,16},{24,20},{28,24},{32,28},{36,32}... | collective-permute-start | bytes 135176 | tf_op jit(solution)/shard_map/ppermute | solution.py:17
  17.0 1.9 collective-permute-start
  20.2 0.9 broadcast_compare_fusion
  21.1 11.7 %all_gather.7 = bf16[256,1408]{0,1:T(8,128)(2,1)S(1)} all-gather(bf16[256,352]{0,1:T(8,128)(2,1)} %param.11), channel_id=1, replica_groups=mesh['dp'=64,'tensor'=4] {'tensor'}, dimensions={1}, use_global_device_ids=true | all-gather | bytes 901120 | tf_op jit(solution)/shard_map/all_gather | solution.py:167
  32.8 1.0 convolution_convert_fusion.2
  34.5 0.6 fusion.40
  35.0 12.8 %all_gather.6 = bf16[256,1408]{0,1:T(8,128)(2,1)S(1)} all-gather(bf16[256,352]{0,1:T(8,128)(2,1)S(1)} %fusion.40), channel_id=1, replica_groups=mesh['dp'=64,'tensor'=4] {'tensor'}, dimensions={1}, use_global_device_ids=true | all-gather | bytes 901120 | tf_op jit(solution)/shard_map/all_gather | solution.py:145
  47.9 0.2 convert_reduce_fusion
  48.1 0.2 fusion.4
  48.4 0.6 fusion.17
  49.3 1.1 fusion.54
  50.3 0.7 fusion.47
  51.1 2.1 fusion.34
  53.2 2.0 convolution_bitcast_fusion
  55.1 2.5 convolution_bitcast_fusion.1
  57.6 2.6 multiply_reduce_fusion.3
  60.2 1.1 multiply_bitcast_fusion.1
  61.3 0.9 maximum_convert_fusion
  62.3 0.7 copy-done.6
  63.0 1.7 convolution_convert_fusion
  64.8 1.2 convolution_convert_fusion.3
  66.0 0.6 copy-done.8
  66.6 2.3 convolution_convert_fusion.1
  69.1 2.4 fusion.71
  71.5 136.0 %fusion = f32[176,24]{0,1:T(8,128)S(1)} fusion(f32[176,1408]{0,1:T(8,128)} %fusion.71), kind=kCustom, calls=%all-reduce-scatter | all-reduce-scatter fusion | flops 270337 | bytes 1009152
  207.5 1.3 collective-permute-start.9
  210.1 0.6 fusion.67
  211.9 1.3 collective-permute-start.8
  213.2 1.3 collective-permute-start.7
  214.5 1.3 collective-permute-start.6
  215.8 1.3 collective-permute-start.5
  217.2 3.7 collective-permute-start.4
  220.9 2.8 fusion.15
  223.7 0.4 collective-permute-done.4
  224.2 0.7 concatenate.32
  225.0 1.3 convert_element_type.94
  226.3 0.4 convert_reduce_fusion.1
  226.7 0.5 copy-done.12
  227.5 4.2 collective-permute-start.3
  231.7 1.9 collective-permute-start.2
  233.6 0.6 dynamic-slice_multiply_fusion.2
  234.2 0.9 collective-permute-done.2
  235.2 1.6 fusion.27
  236.8 1.6 add_convert_fusion
  238.4 186.4 %all-reduce.10.cloned.1.call-done = f32[3,176,1408]{1,2,0:T(8,128)} async-done(((f32[3,176,1408]{1,2,0:T(8,128)}), f32[3,176,1408]{1,2,0:T(8,128)}) %all-reduce.10.cloned.1.call-update) | async-done | bytes 2973712
  424.8 1.5 dynamic-slice_multiply_fusion.1
  (68 shorter events, 0.9 us)
Async XLA Ops:
  7.2 41.2 %copy-start = (bf16[3,176,1408]{2,1,0:T(8,128)(2,1)S(1)}, bf16[3,176,1408]{2,1,0:T(8,128)(2,1)}, u32[]{:S(2)}) copy-start(bf16[3,176,1408]{2,1,0:T(8,128)(2,1)} %param.9) | copy-start | bytes 4460548
  7.2 25.6 %copy-start.2 = (bf16[176,1408]{1,0:T(8,128)(2,1)S(1)}, bf16[176,1408]{1,0:T(8,128)(2,1)}, u32[]{:S(2)}) copy-start(bf16[176,1408]{1,0:T(8,128)(2,1)} %param.10) | copy-start | bytes 1486852
  7.2 217.7 %all-reduce.8.cloned.1.call-start = ((), (), s32[]{:S(2)}) async-start(), calls=%async_computation.2 | async-start | bytes 1441792 | tf_op jit(solution)/shard_map/psum | solution.py:196
  10.6 23.1 %copy-start.9 = (bf16[64,352]{0,1:T(8,128)(2,1)}, bf16[64,352]{0,1:T(8,128)(2,1)S(1)}, u32[]{:S(2)}) copy-start(bf16[64,352]{0,1:T(8,128)(2,1)S(1)} %broadcast.159) | copy-start | bytes 135172
  10.6 23.8 %copy-start.5 = (bf16[384,352]{0,1:T(8,128)(2,1)S(1)}, bf16[384,352]{0,1:T(8,128)(2,1)}, u32[]{:S(2)}) copy-start(bf16[384,352]{0,1:T(8,128)(2,1)} %param.6) | copy-start | bytes 811012
  11.8 22.6 %collective-permute-start.1 = (bf16[64,352]{0,1:T(8,128)(2,1)S(1)}, bf16[64,352]{0,1:T(8,128)(2,1)S(1)}, u32[]{:S(2)}, u32[]{:S(2)}) collective-permute-start(bf16[64,352]{0,1:T(8,128)(2,1)S(1)} %get-tuple-element.70), channel_id=1, source_target_pairs={{4,0},{8,4},{12,8},{16,12},{20,16},{24,20},{28,24},{32,28},{36,32}... | collective-permute-start | bytes 135176 | tf_op jit(solution)/shard_map/ppermute | solution.py:17
  17.0 17.5 %collective-permute-start = (bf16[64,352]{0,1:T(8,128)(2,1)S(1)}, bf16[64,352]{0,1:T(8,128)(2,1)S(1)}, u32[]{:S(2)}, u32[]{:S(2)}) collective-permute-start(bf16[64,352]{0,1:T(8,128)(2,1)S(1)} %get-tuple-element.71), channel_id=1, source_target_pairs={{0,4},{4,8},{8,12},{12,16},{16,20},{20,24},{24,28},{28,32},{32,36}... | collective-permute-start | bytes 135176 | tf_op jit(solution)/shard_map/ppermute | solution.py:17
  35.0 13.3 %copy-start.3 = (bf16[256,352]{0,1:T(8,128)(2,1)}, bf16[256,352]{0,1:T(8,128)(2,1)S(1)}, u32[]{:S(2)}) copy-start(bf16[256,352]{0,1:T(8,128)(2,1)S(1)} %fusion.40) | copy-start | bytes 540676
  48.1 0.9 copy-start.13
  48.4 0.9 copy-start.11
  62.3 0.7 copy-start.6
  64.7 172.0 %reduce-scatter.5.cloned.1.call-start = ((), (), s32[]{:S(2)}) async-start(), calls=%async_computation.1 | async-start | bytes 901120 | tf_op jit(solution)/shard_map/reduce_scatter | solution.py:163
  66.0 0.6 copy-start.8
  69.0 355.8 %all-reduce.10.cloned.1.call-start = ((), (), s32[]{:S(2)}) async-start(), calls=%async_computation.3 | async-start | bytes 8650752
  69.1 141.0 %copy-start.15 = (u32[256]{0:T(256)S(1)}, u32[256]{0:T(256)}, u32[]{:S(2)}) copy-start(u32[256]{0:T(256)} %constant.117) | copy-start | bytes 3076
  69.1 151.8 %copy-start.7 = (bf16[256,3,2,88]{0,3,2,1:T(8,128)(2,1)S(1)}, bf16[256,3,2,88]{0,3,2,1:T(8,128)(2,1)}, u32[]{:S(2)}) copy-start(bf16[256,3,2,88]{0,3,2,1:T(8,128)(2,1)} %copy-done.6) | copy-start | bytes 811012
  69.1 151.8 %copy-start.14 = (f32[256]{0:T(256)S(1)}, f32[256]{0:T(256)}, u32[]{:S(2)}) copy-start(f32[256]{0:T(256)} %copy-done.13) | copy-start | bytes 3076
  207.5 9.7 %collective-permute-start.9 = (f32[176,6]{0,1:T(8,128)S(1)}, f32[176,6]{0,1:T(8,128)S(1)}, u32[]{:S(2)}, u32[]{:S(2)}) collective-permute-start(f32[176,6]{0,1:T(8,128)S(1)} %slice.24), channel_id=1, source_target_pairs={{0,24},{4,28},{8,32},{12,36},{16,40},{20,44},{24,48},{28,52},{32,5... | collective-permute-start | bytes 12680
  211.9 11.7 %collective-permute-start.8 = (f32[176,24]{0,1:T(8,128)S(1)}, f32[176,24]{0,1:T(8,128)S(1)}, u32[]{:S(2)}, u32[]{:S(2)}) collective-permute-start(f32[176,24]{0,1:T(8,128)S(1)} %fusion), channel_id=1, source_target_pairs={{0,20},{4,24},{8,28},{12,32},{16,36},{20,40},{24,44},{28,48},{32,5... | collective-permute-start | bytes 50696
  213.2 10.4 %collective-permute-start.7 = (f32[176,24]{0,1:T(8,128)S(1)}, f32[176,24]{0,1:T(8,128)S(1)}, u32[]{:S(2)}, u32[]{:S(2)}) collective-permute-start(f32[176,24]{0,1:T(8,128)S(1)} %fusion), channel_id=1, source_target_pairs={{0,16},{4,20},{8,24},{12,28},{16,32},{20,36},{24,40},{28,44},{32,4... | collective-permute-start | bytes 50696
  214.5 9.1 %collective-permute-start.6 = (f32[176,24]{0,1:T(8,128)S(1)}, f32[176,24]{0,1:T(8,128)S(1)}, u32[]{:S(2)}, u32[]{:S(2)}) collective-permute-start(f32[176,24]{0,1:T(8,128)S(1)} %fusion), channel_id=1, source_target_pairs={{0,12},{4,16},{8,20},{12,24},{16,28},{20,32},{24,36},{28,40},{32,4... | collective-permute-start | bytes 50696
  215.8 7.9 %collective-permute-start.5 = (f32[176,24]{0,1:T(8,128)S(1)}, f32[176,24]{0,1:T(8,128)S(1)}, u32[]{:S(2)}, u32[]{:S(2)}) collective-permute-start(f32[176,24]{0,1:T(8,128)S(1)} %fusion), channel_id=1, source_target_pairs={{0,8},{4,12},{8,16},{12,20},{16,24},{20,28},{24,32},{28,36},{32,40... | collective-permute-start | bytes 50696
  217.2 7.0 %collective-permute-start.4 = (f32[176,24]{0,1:T(8,128)S(1)}, f32[176,24]{0,1:T(8,128)S(1)}, u32[]{:S(2)}, u32[]{:S(2)}) collective-permute-start(f32[176,24]{0,1:T(8,128)S(1)} %fusion), channel_id=1, source_target_pairs={{0,4},{4,8},{8,12},{12,16},{16,20},{20,24},{24,28},{28,32},{32,36}... | collective-permute-start | bytes 50696
  224.9 1.3 copy-start.1
  226.3 0.9 copy-start.12
  226.3 1.0 copy-start.10
  226.7 10.1 %copy-start.4 = (bf16[256,352]{0,1:T(8,128)(2,1)S(1)}, bf16[256,352]{0,1:T(8,128)(2,1)}, u32[]{:S(2)}) copy-start(bf16[256,352]{0,1:T(8,128)(2,1)} %copy-done.3) | copy-start | bytes 540676
  227.5 6.7 %collective-permute-start.3 = (bf16[64,352]{0,1:T(8,128)(2,1)S(1)}, bf16[64,352]{0,1:T(8,128)(2,1)S(1)}, u32[]{:S(2)}, u32[]{:S(2)}) collective-permute-start(bf16[64,352]{0,1:T(8,128)(2,1)S(1)} %get-tuple-element.72), channel_id=1, source_target_pairs={{4,0},{8,4},{12,8},{16,12},{20,16},{24,20},{28,24},{32,28},{36,32}... | collective-permute-start | bytes 135176 | tf_op jit(solution)/shard_map/ppermute | solution.py:17
  231.7 3.5 collective-permute-start.2
Sparse Core Ops, SparseCore 0:
  64.8 52.0 all-reduce.7
  119.5 26.2 reduce-scatter.4
  223.8 200.9 all-reduce.9
where the time goes:
time: 435 us; the launch traced here: 433 us
  waiting for transfers between devices  188 us (43%)
  blocking collectives  161 us (37%)
  starting transfers between devices  23.4 us (5%)
  matrix products  22.2 us (5%)
  between operations  20.7 us (5%)
  other arithmetic  13.4 us (3%)
  local copies, waits for them, and re-layouts  4.85 us (1%)
    unnamed x10, waiting for transfers between devices  187 us
    unnamed x1, blocking collectives  136 us
    ppermute x4, starting transfers between devices, from_behind(): return lax.ppermute(block, axis, route)  13.1 us
    all_gather x1, blocking collectives, layer_pass(): full_rows = lax.all_gather(columns, 'tensor', axis=1, tiled=True)  12.8 us
    all_gather x1, blocking collectives, layer_pass(): grad_full = lax.all_gather(grad_columns, 'tensor', axis=1, tiled=True)  11.7 us
    unnamed x7, starting transfers between devices  10.2 us
  transfers between devices with their start and end apart: 13, of which 3 were waited for; matrix products, arithmetic and copies ran while one was open for 36% of the time, Pallas kernels for 0%

commit v1 on v0

v1 whole, which is shorter than its diff:
```python
import math

import jax
import jax.numpy as jnp
from jax import lax
from jax.experimental import pallas as pl
from jax.experimental.pallas import tpu as pltpu
from jax.sharding import PartitionSpec as P

HD = 88
PAD = 128
SEQ = 256
SRC = 384
SPILL = 64
COLS = 352
MODEL = 1408
QW = 176
HALF = 384
NT = 4
NX = 4
NZ = 8
SHARE = 22
CORE_ROWS = 24
norm_eps = 1e-06
score_scale = HD ** (-0.5)
total_scale = 1.0 / math.sqrt(16384.0)

BF = jnp.bfloat16
F32 = jnp.float32
MESH = pl.DeviceIdType.MESH


def dot(a, b, ca=1, cb=0):
    return lax.dot_general(a, b, (((ca,), (cb,)), ((), ())), preferred_element_type=F32)


def grid2(rows, cols):
    r = lax.broadcasted_iota(jnp.int32, (rows, cols), 0)
    c = lax.broadcasted_iota(jnp.int32, (rows, cols), 1)
    return r, c


def hot(mask):
    return jnp.where(mask, 1.0, 0.0).astype(BF)


def kernel(
    cut_ref, seg_ref, patches_ref, wqkv_ref, wout_ref, gout_ref,
    mixed_ref, gpatch_ref, gqkv_ref, gwout_ref,
    go_full, x_full, n_low, n_t, go_t, w_pad, wo_pad,
    snd_next, from_prev, from_next, bsnd_next, bfrom_prev, bfrom_next, gx,
    rs_send, rs_rin, rs_fin, share, right_side, h_send, h_recv, h_keep,
    xs_send, xs_rin, xs_fin, z_send, z_recv, t_buf, f_recv,
    ssem, rsem,
):
    d = lax.axis_index("dp")
    t = lax.axis_index("tensor")
    xi = d // 16
    zi = lax.rem(d // 2, NZ)
    core = lax.rem(d, 2)
    inner = lax.rem(d, 16)
    t_right, t_left, t_far = lax.rem(t + 1, NT), lax.rem(t + 3, NT), lax.rem(t + 2, NT)
    x_right, x_left, x_far = lax.rem(xi + 1, NX), lax.rem(xi + 3, NX), lax.rem(xi + 2, NX)
    dp_next = (lax.rem(d + 1, 64), t)
    dp_prev = (lax.rem(d + 63, 64), t)
    mate = (d + 1 - 2 * core, t)
    y_right, y_left = (d, t_right), (d, t_left)
    px_right, px_left = (x_right * 16 + inner, t), (x_left * 16 + inner, t)
    z_peers = [
        (lax.rem(zi + k, NZ), (xi * 16 + lax.rem(zi + k, NZ) * 2 + core, t)) for k in range(1, NZ)
    ]

    barrier = pltpu.get_barrier_semaphore()
    greet = [dp_next, dp_prev, y_right, y_left, px_right, px_left] + [p for _, p in z_peers]
    for peer in greet:
        pl.semaphore_signal(barrier, inc=1, device_id=peer, device_id_type=MESH)

    counter = [0]
    pending = []

    def remote(src, dst, dev):
        k = counter[0]
        counter[0] += 1
        copy = pltpu.make_async_remote_copy(
            src_ref=src, dst_ref=dst, send_sem=ssem.at[k], recv_sem=rsem.at[k],
            device_id=dev, device_id_type=MESH,
        )
        copy.start()
        pending.append(copy)
        return copy

    lower = cut_ref[0, 0]
    upper = cut_ref[0, 1]
    head = jnp.maximum(lower, 0)
    tail = jnp.maximum(-upper, 0)

    r, c = grid2(SPILL, SRC)
    base = SEQ - lower + jnp.minimum(upper, 0)
    snd_next[...] = dot(hot(c == r + base), patches_ref[...]).astype(BF)

    pl.semaphore_wait(barrier, len(greet))

    to_next = remote(snd_next, from_prev, dp_next)
    to_prev = remote(patches_ref.at[pl.ds(0, SPILL)], from_next, dp_prev)

    half = SEQ // 2
    lo, hi = pl.ds(0, half), pl.ds(half, half)

    def gather_start(src, full):
        ra = remote(src.at[lo], full.at[t, lo], y_right)
        lb = remote(src.at[hi], full.at[t, hi], y_left)
        rb = remote(src.at[hi], full.at[t, hi], y_right)
        la = remote(src.at[lo], full.at[t, lo], y_left)
        return ra, lb, rb, la

    def gather_relay(full, first):
        ra, lb, rb, la = first
        ra.wait_recv()
        fa = remote(full.at[t_left, lo], full.at[t_left, lo], y_right)
        lb.wait_recv()
        fb = remote(full.at[t_right, hi], full.at[t_right, hi], y_left)
        return rb, la, fa, fb

    def gather_finish(rest):
        for copy in rest:
            copy.wait_recv()

    go_first = gather_start(gout_ref, go_full)
    go_full[t] = gout_ref[...]

    r, c = grid2(SEQ, SRC)
    mine = (c == r - lower) & (r >= head) & (r < SEQ - tail)
    own = dot(hot(mine), patches_ref[...])
    r, c = grid2(SEQ, SPILL)
    pick_prev = hot((c == r) & (r < head))
    pick_next = hot((c == r - (SEQ - tail)) & (r >= SEQ - tail))
    to_next.wait_recv()
    to_prev.wait_recv()
    own = own + dot(pick_prev, from_prev[...]) + dot(pick_next, from_next[...])
    x_full[t] = own.astype(BF)
    x_first = gather_start(x_full.at[t], x_full)
    go_rest = gather_relay(go_full, go_first)

    r, c = grid2(2 * PAD, QW)
    pad_rows = hot(((r < PAD) & (c == r) & (c < HD)) | ((r >= PAD) & (c == r - PAD + HD) & (c >= HD)))
    for u in range(NT):
        span = slice(u * COLS, (u + 1) * COLS)
        for part in range(3):
            w_pad[u, part * 256 : (part + 1) * 256, :] = dot(
                pad_rows, wqkv_ref[part, :, span]
            ).astype(BF)
        wo_pad[u] = dot(pad_rows, wout_ref[:, span]).astype(BF)

    x_rest = gather_relay(x_full, x_first)

    r, c = grid2(COLS, COLS)
    eye = hot(r == c)
    gather_finish(go_rest)
    grad_att = jnp.zeros((SEQ, 2 * PAD), F32)
    for u in range(NT):
        grad_att = grad_att + dot(go_full[u], wo_pad[u], 1, 1)
        go_t[u] = dot(eye, go_full[u], 1, 1).astype(BF)
    grad_att = grad_att.astype(BF)

    gather_finish(x_rest)
    mean = jnp.zeros((SEQ, 1), F32)
    for u in range(NT):
        mean = mean + jnp.sum(x_full[u].astype(F32), axis=-1, keepdims=True)
    mean = mean * (1.0 / MODEL)
    spread = jnp.zeros((SEQ, 1), F32)
    for u in range(NT):
        center = x_full[u].astype(F32) - mean
        spread = spread + jnp.sum(center * center, axis=-1, keepdims=True)
    rstd = lax.rsqrt(spread * (1.0 / MODEL) + norm_eps)
    proj = jnp.zeros((SEQ, 6 * PAD), F32)
    for u in range(NT):
        low = ((x_full[u].astype(F32) - mean) * rstd).astype(BF)
        n_low[u] = low
        proj = proj + dot(low, w_pad[u], 1, 1)

    live = lax.broadcasted_iota(jnp.int32, (SEQ, PAD), 1) < HD

    def head_norm(v):
        center = jnp.where(live, v - jnp.sum(v, axis=-1, keepdims=True) * (1.0 / HD), 0.0)
        var = jnp.sum(center * center, axis=-1, keepdims=True) * (1.0 / HD)
        inverse = lax.rsqrt(var + norm_eps)
        return center * inverse, inverse

    def head_back(g, normed, inverse):
        first = jnp.sum(g, axis=-1, keepdims=True) * (1.0 / HD)
        second = jnp.sum(g * normed, axis=-1, keepdims=True) * (1.0 / HD)
        return jnp.where(live, inverse * (g - first - normed * second), 0.0)

    seg_row = seg_ref[...].astype(F32)
    r, c = grid2(SEQ, SEQ)
    seg_col = jnp.sum(jnp.where(r == c, seg_row, 0.0), axis=-1, keepdims=True)
    same = seg_col == seg_row

    saved = []
    att_parts = []
    for h in range(2):
        q_hat, q_inv = head_norm(proj[:, h * PAD : (h + 1) * PAD])
        k_hat, k_inv = head_norm(proj[:, (2 + h) * PAD : (3 + h) * PAD])
        v = proj[:, (4 + h) * PAD : (5 + h) * PAD].astype(BF)
        q, k = q_hat.astype(BF), k_hat.astype(BF)
        raised = jnp.where(same, jnp.exp(dot(q, k, 1, 1) * score_scale), 0.0)
        weights = raised / jnp.sum(raised, axis=-1, keepdims=True)
        weights_low = weights.astype(BF)
        att_parts.append(dot(weights_low, v).astype(BF))
        saved.append((q_hat, q_inv, k_hat, k_inv, q, k, v, weights, weights_low))
    att = jnp.concatenate(att_parts, axis=1)

    def scatter_start(send, rin, make, far, right, left, to_right, to_left, cut_at):
        a, b = pl.ds(0, cut_at), pl.ds(cut_at, cut_at)
        send[0] = make(far).astype(BF)
        ra = remote(send.at[0, a], rin.at[0], to_right)
        lb = remote(send.at[0, b], rin.at[1], to_left)
        return ra, lb

    def scatter_plain(send, fin, make, right, left, to_right, to_left, cut_at):
        a, b = pl.ds(0, cut_at), pl.ds(cut_at, cut_at)
        send[1] = make(right).astype(BF)
        rb = remote(send.at[1, b], fin.at[0, b], to_right)
        send[2] = make(left).astype(BF)
        la = remote(send.at[2, a], fin.at[1, a], to_left)
        return rb, la

    def scatter_relay(send, rin, fin, first, plain, to_right, to_left, cut_at):
        a, b = pl.ds(0, cut_at), pl.ds(cut_at, cut_at)
        ra, lb = first
        rb, la = plain
        ra.wait_recv()
        send[1, a] = (send[1, a].astype(F32) + rin[0].astype(F32)).astype(BF)
        fa = remote(send.at[1, a], fin.at[0, a], to_right)
        lb.wait_recv()
        send[2, b] = (send[2, b].astype(F32) + rin[1].astype(F32)).astype(BF)
        fb = remote(send.at[2, b], fin.at[1, b], to_left)
        return rb, la, fa, fb

    def branch(u):
        return dot(att, wo_pad[u])

    b_send, b_rin, b_fin = rs_send.at[0], rs_rin.at[0], rs_fin.at[0]
    b_first = scatter_start(b_send, b_rin, branch, t_far, t_right, t_left, y_right, y_left, half)
    b_plain = scatter_plain(b_send, b_fin, branch, t_right, t_left, y_right, y_left, half)
    mixed_own = x_full[t].astype(F32) + branch(t)

    grads = {}
    for h in range(2):
        q_hat, q_inv, k_hat, k_inv, q, k, v, weights, weights_low = saved[h]
        ga = grad_att[:, h * PAD : (h + 1) * PAD]
        gw = dot(ga, v, 1, 1)
        inner_sum = jnp.sum(gw * weights, axis=-1, keepdims=True)
        gs = (weights * (gw - inner_sum) * score_scale).astype(BF)
        gq = dot(gs, k)
        gk = dot(gs, q, 0, 0)
        gv = dot(weights_low, ga, 0, 0)
        grads[0, h] = head_back(gq, q_hat, q_inv).astype(BF)
        grads[1, h] = head_back(gk, k_hat, k_inv).astype(BF)
        grads[2, h] = gv.astype(BF)
    gp = jnp.concatenate([grads[p, h] for p in range(3) for h in range(2)], axis=1)

    b_rest = scatter_relay(b_send, b_rin, b_fin, b_first, b_plain, y_right, y_left, half)

    r, c = grid2(4 * PAD, HALF)
    squeeze = c == -1
    for a in range(4):
        squeeze = squeeze | ((r - a * PAD == c - a * HD) & (r >= a * PAD) & (r < a * PAD + HD))
    squeeze = hot(squeeze)
    right_side[0, 0:SEQ, :] = dot(gp[:, 0 : 4 * PAD], squeeze).astype(BF)
    right_side[0, SEQ : 2 * SEQ, :] = jnp.zeros((SEQ, HALF), BF)
    right_side[1, 0:SEQ, :] = dot(gp[:, 4 * PAD : 6 * PAD], squeeze[0 : 2 * PAD]).astype(BF)
    right_side[1, SEQ : 2 * SEQ, :] = dot(att, squeeze[2 * PAD : 4 * PAD]).astype(BF)

    order = [x_far, x_right, x_left, xi]
    for u in range(NT):
        n_t[u] = dot(eye, n_low[u], 1, 1).astype(BF)

    def weight_grad(u, side):
        return dot(n_t[u], right_side[side, 0:SEQ, :]) + dot(
            go_t[u], right_side[side, SEQ : 2 * SEQ, :]
        )

    h_copies = []
    for u in order:
        h_send[u] = weight_grad(u, 1 - core).astype(BF)
        h_copies.append(remote(h_send.at[u], h_recv.at[u], mate))

    s1 = jnp.zeros((SEQ, 1), F32)
    s2 = jnp.zeros((SEQ, 1), F32)
    for u in range(NT):
        part = dot(gp, w_pad[u])
        share[u] = part
        s1 = s1 + jnp.sum(part, axis=-1, keepdims=True)
        s2 = s2 + jnp.sum(
            part * ((x_full[u].astype(F32) - mean) * rstd), axis=-1, keepdims=True
        )
    s1 = s1 * (1.0 / MODEL)
    s2 = s2 * (1.0 / MODEL)

    def back(u):
        return rstd * (share[u] - s1 - ((x_full[u].astype(F32) - mean) * rstd) * s2)

    g_send, g_rin, g_fin = rs_send.at[1], rs_rin.at[1], rs_fin.at[1]
    g_first = scatter_start(g_send, g_rin, back, t_far, t_right, t_left, y_right, y_left, half)
    g_plain = scatter_plain(g_send, g_fin, back, t_right, t_left, y_right, y_left, half)

    for u in order:
        h_keep[u] = weight_grad(u, core)

    def pair(u):
        return h_keep[u] + h_recv[u].astype(F32)

    cut_x = COLS // 2
    h_copies[0].wait_recv()
    x_fst = scatter_start(xs_send, xs_rin, pair, x_far, x_right, x_left, px_right, px_left, cut_x)
    h_copies[1].wait_recv()
    h_copies[2].wait_recv()
    x_pln = scatter_plain(xs_send, xs_fin, pair, x_right, x_left, px_right, px_left, cut_x)

    gx_own = gout_ref[...].astype(F32) + back(t)

    for copy in b_rest:
        copy.wait_recv()
    mixed_ref[...] = (mixed_own + b_fin[0].astype(F32) + b_fin[1].astype(F32)).astype(BF)

    g_rest = scatter_relay(g_send, g_rin, g_fin, g_first, g_plain, y_right, y_left, half)
    x_rst = scatter_relay(xs_send, xs_rin, xs_fin, x_fst, x_pln, px_right, px_left, cut_x)
    h_copies[3].wait_recv()

    for copy in g_rest:
        copy.wait_recv()
    gx[...] = (gx_own + g_fin[0].astype(F32) + g_fin[1].astype(F32)).astype(BF)
    r, c = grid2(SPILL, SEQ)
    bsnd_next[...] = dot(hot(c == r + SEQ - tail), gx[...]).astype(BF)
    back_next = remote(bsnd_next, bfrom_prev, dp_next)
    back_prev = remote(gx.at[pl.ds(0, SPILL)], bfrom_next, dp_prev)

    for copy in x_rst:
        copy.wait_recv()
    summed = (pair(xi) + xs_fin[0].astype(F32) + xs_fin[1].astype(F32)).astype(BF)
    block = 2 * CORE_ROWS
    for k in range(NZ):
        r, c = grid2(block, COLS)
        first = (r < SHARE) & (c == r + 2 * k * SHARE)
        second = (r >= CORE_ROWS) & (r < CORE_ROWS + SHARE)
        second = second & (c == r - CORE_ROWS + (2 * k + 1) * SHARE)
        z_send[k] = dot(hot(first | second), summed).astype(BF)
    z_copies = [remote(z_send.at[pz], z_recv.at[zi], dev) for pz, dev in z_peers]

    length = SEQ + upper - lower
    behind = jnp.maximum(-lower, 0)
    ahead = jnp.maximum(upper, 0)
    r, c = grid2(SRC, SEQ)
    mine = hot((c == r + lower) & (r >= behind) & (r < length - ahead))
    src_rows = dot(mine, gx[...])
    r, c = grid2(SRC, SPILL)
    pick_prev = hot((c == r) & (r < behind))
    pick_next = hot((c == r - (length - ahead)) & (r >= length - ahead) & (r < length))
    back_next.wait_recv()
    back_prev.wait_recv()
    src_rows = src_rows + dot(pick_prev, bfrom_prev[...]) + dot(pick_next, bfrom_next[...])
    gpatch_ref[...] = src_rows.astype(BF)

    total = z_send[zi].astype(F32)
    for copy in z_copies:
        copy.wait_recv()
    for pz, _ in z_peers:
        total = total + z_recv[pz].astype(F32)
    total = total * total_scale
    t_buf[0] = total[0:CORE_ROWS]
    t_buf[1] = total[CORE_ROWS : 2 * CORE_ROWS]
    last = remote(t_buf.at[1 - core], f_recv, mate)
    kept = t_buf[core]
    last.wait_recv()
    got = f_recv[...]
    qk = jnp.where(core == 0, kept, got)
    vo = jnp.where(core == 0, got, kept)
    fill = jnp.zeros((PAD - CORE_ROWS, HALF), F32)
    qk = jnp.transpose(jnp.concatenate([qk, fill], axis=0))
    vo = jnp.transpose(jnp.concatenate([vo, fill], axis=0))
    gqkv_ref[0] = qk[0:QW, 0:SHARE]
    gqkv_ref[1] = qk[QW : 2 * QW, 0:SHARE]
    gqkv_ref[2] = vo[0:QW, 0:SHARE]
    gwout_ref[...] = vo[QW : 2 * QW, 0:SHARE]

    for copy in pending:
        copy.wait_send()


COPIES = 48


def body(patches, seg_ids, cut, w_qkv, w_out, grad_out):
    vmem = pl.BlockSpec(memory_space=pltpu.VMEM)
    smem = pl.BlockSpec(memory_space=pltpu.SMEM)
    scratch = [
        pltpu.VMEM((NT, SEQ, COLS), BF),
        pltpu.VMEM((NT, SEQ, COLS), BF),
        pltpu.VMEM((NT, SEQ, COLS), BF),
        pltpu.VMEM((NT, COLS, SEQ), BF),
        pltpu.VMEM((NT, COLS, SEQ), BF),
        pltpu.VMEM((NT, 6 * PAD, COLS), BF),
        pltpu.VMEM((NT, 2 * PAD, COLS), BF),
        pltpu.VMEM((SPILL, COLS), BF),
        pltpu.VMEM((SPILL, COLS), BF),
        pltpu.VMEM((SPILL, COLS), BF),
        pltpu.VMEM((SPILL, COLS), BF),
        pltpu.VMEM((SPILL, COLS), BF),
        pltpu.VMEM((SPILL, COLS), BF),
        pltpu.VMEM((SEQ, COLS), BF),
        pltpu.VMEM((2, 3, SEQ, COLS), BF),
        pltpu.VMEM((2, 2, SEQ // 2, COLS), BF),
        pltpu.VMEM((2, 2, SEQ, COLS), BF),
        pltpu.VMEM((NT, SEQ, COLS), F32),
        pltpu.VMEM((2, 2 * SEQ, HALF), BF),
        pltpu.VMEM((NT, COLS, HALF), BF),
        pltpu.VMEM((NT, COLS, HALF), BF),
        pltpu.VMEM((NT, COLS, HALF), F32),
        pltpu.VMEM((3, COLS, HALF), BF),
        pltpu.VMEM((2, COLS // 2, HALF), BF),
        pltpu.VMEM((2, COLS, HALF), BF),
        pltpu.VMEM((NZ, 2 * CORE_ROWS, HALF), BF),
        pltpu.VMEM((NZ, 2 * CORE_ROWS, HALF), BF),
        pltpu.VMEM((2, CORE_ROWS, HALF), F32),
        pltpu.VMEM((CORE_ROWS, HALF), F32),
        pltpu.SemaphoreType.DMA((COPIES,)),
        pltpu.SemaphoreType.DMA((COPIES,)),
    ]
    return pl.pallas_call(
        kernel,
        out_shape=(
            jax.ShapeDtypeStruct((SEQ, COLS), BF),
            jax.ShapeDtypeStruct((SRC, COLS), BF),
            jax.ShapeDtypeStruct((3, QW, SHARE), F32),
            jax.ShapeDtypeStruct((QW, SHARE), F32),
        ),
        in_specs=[smem, vmem, vmem, vmem, vmem, vmem],
        out_specs=(vmem, vmem, vmem, vmem),
        scratch_shapes=scratch,
        compiler_params=pltpu.CompilerParams(
            collective_id=0, has_side_effects=True, vmem_limit_bytes=56 * 1024 * 1024
        ),
    )(cut, seg_ids.reshape(1, SEQ), patches, w_qkv, w_out, grad_out)


def solution(mesh):
    in_specs = (
        P("dp", "tensor"),
        P("dp"),
        P("dp", None),
        P(None, "tensor", None),
        P("tensor", None),
        P("dp", "tensor"),
    )
    out_specs = (P("dp", "tensor"), P("dp", "tensor"), P(None, "tensor", "dp"), P("tensor", "dp"))
    return jax.shard_map(body, mesh=mesh, in_specs=in_specs, out_specs=out_specs, check_vma=False)
```

time: 435 us -> 70.4 us (0.16)
  waiting for transfers between devices: 188 us -> 0 us
  blocking collectives: 161 us -> 0 us
  Pallas kernels: 0 us -> 59.1 us
  starting transfers between devices: 23.4 us -> 0 us
  matrix products: 22.2 us -> 0 us
  between operations: 20.7 us -> 0.64 us
  other arithmetic: 13.4 us -> 0 us
  local copies, waits for them, and re-layouts: 4.85 us -> 10.4 us
    unnamed x10 -> x0, waiting for transfers between devices: 187 us -> none
    unnamed x1 -> x0, blocking collectives: 136 us -> none
    pallas_call x0 -> x1, Pallas kernels: none -> 59.1 us  [body(): pl.pallas_call(kernel, out_shape=(jax.ShapeDtypeStruct((SEQ, COLS), BF),...]
    all_gather x2 -> x0, blocking collectives: 24.6 us -> none  [the longest x1 12.8 us: layer_pass(): full_rows = lax.all_gather(columns, 'tensor', axis=1, tiled=True)]
    dot_general x11 -> x0, matrix products: 20.1 us -> none  [the longest x1 2.76 us: layer_pass(): jnp.einsum('rc,rd->cd', grad_proj, normed_low, preferred_element_type=jnp...]
    ppermute x4 -> x0, starting transfers between devices: 13.1 us -> none  [from_behind(): return lax.ppermute(block, axis, route)]
    unnamed x7 -> x0, starting transfers between devices: 10.2 us -> none
    pallas_call x0 -> x4, local copies, waits for them, and re-layouts: none -> 6.88 us  [body(): pl.pallas_call(kernel, out_shape=(jax.ShapeDtypeStruct((SEQ, COLS), BF),...]
  transfers between devices with their start and end apart: 13 -> 0, of which waited for: 3 -> 0; matrix products, arithmetic and copies ran while one was open for 36% -> 0% of each run, Pallas kernels for 0% -> 0%
where the time goes in v1:
time: 70.4 us; the launch traced here: 70.2 us
  Pallas kernels  59.1 us (84%)
  local copies, waits for them, and re-layouts  10.4 us (15%)
    pallas_call x1, Pallas kernels, body(): pl.pallas_call(kernel, out_shape=(jax.ShapeDtypeStruct((SEQ, COLS), BF),...  59.1 us
    pallas_call x4, local copies, waits for them, and re-layouts, body(): pl.pallas_call(kernel, out_shape=(jax.ShapeDtypeStruct((SEQ, COLS), BF),...  6.88 us
    unnamed x2, local copies, waits for them, and re-layouts  3.57 us

profile of v1, /device:TPU:1, one launch (start us, length us, event | category | flops | bytes accessed | tf_op | source)
XLA Modules:
  0.0 70.2 jit_solution(5181925835991946420)
XLA Ops:
  0.6 1.7 %copy.11.gout_ref = bf16[256,352]{1,0:T(8,128)(2,1)} copy(bf16[256,352]{0,1:T(8,128)(2,1)} %param.11) | data formatting | bytes 360448 | tf_op args[5]
  2.4 1.8 %copy.10.patches_ref = bf16[384,352]{1,0:T(8,128)(2,1)} copy(bf16[384,352]{0,1:T(8,128)(2,1)} %param.6) | data formatting | bytes 540672 | tf_op args[0]
  4.2 59.1 %shard_map.93 = (bf16[256,352]{1,0:T(8,128)(2,1)}, bf16[384,352]{1,0:T(8,128)(2,1)}, f32[3,176,22]{2,1,0:T(8,128)}, f32[176,22]{1,0:T(8,128)}) custom-call(s32[1,2]{1,0:T(1,128)} %cut_ref.1, s32[1,256]{1,0:T(1,128)} %bitcast.1, bf16[384,352]{1,0:T(8,128)(2,1)} %copy.10.patches_ref, bf16[3,176,1408]{2,1,0:T(8,128)(2,1)} %wqkv_ref.1, ...), custom_call_target="tpu_custom_call" | custom-call | tf_op jit(solution)/shard_map/pallas_call | solution.py:430
  63.3 1.7 %copy.12 = bf16[256,352]{0,1:T(8,128)(2,1)} copy(bf16[256,352]{1,0:T(8,128)(2,1)} %get-tuple-element.4) | data formatting | bytes 360448 | tf_op jit(solution)/shard_map/pallas_call | solution.py:430
  65.0 1.6 %copy.15 = f32[176,22]{0,1:T(8,128)} copy(f32[176,22]{1,0:T(8,128)} %get-tuple-element.7) | data formatting | bytes 30976 | tf_op jit(solution)/shard_map/pallas_call | solution.py:430
  66.6 1.7 %copy.14 = f32[3,176,22]{1,2,0:T(8,128)} copy(f32[3,176,22]{2,1,0:T(8,128)} %get-tuple-element.6) | data formatting | bytes 92928 | tf_op jit(solution)/shard_map/pallas_call | solution.py:430
  68.3 1.8 %copy.13 = bf16[384,352]{0,1:T(8,128)(2,1)} copy(bf16[384,352]{1,0:T(8,128)(2,1)} %get-tuple-element.5) | data formatting | bytes 540672 | tf_op jit(solution)/shard_map/pallas_call | solution.py:430

commit v2 on v1

v2 whole, which is shorter than its diff:
```python
import math

import jax
import jax.numpy as jnp
from jax import lax
from jax.experimental import pallas as pl
from jax.experimental.pallas import tpu as pltpu
from jax.sharding import PartitionSpec as P

HD = 88
SEQ = 256
SRC = 384
SPILL = 64
COLS = 352
MODEL = 1408
QW = 176
NT = 4
NX = 4
NZ = 8
SHARE = 22
CORE_ROWS = 24
norm_eps = 1e-06
score_scale = HD ** (-0.5)
total_scale = 1.0 / math.sqrt(16384.0)

BF = jnp.bfloat16
F32 = jnp.float32
MESH = pl.DeviceIdType.MESH


def dot(a, b, ca=1, cb=0):
    return lax.dot_general(a, b, (((ca,), (cb,)), ((), ())), preferred_element_type=F32)


def grid2(rows, cols):
    r = lax.broadcasted_iota(jnp.int32, (rows, cols), 0)
    c = lax.broadcasted_iota(jnp.int32, (rows, cols), 1)
    return r, c


def hot(mask):
    return jnp.where(mask, 1.0, 0.0).astype(BF)


def kernel(
    cut_ref, seg_ref, patches_ref, wqkv_ref, wout_ref, gout_ref,
    mixed_ref, gpatch_ref, gqkv_ref, gwout_ref,
    acts, x_full, w_t, wo_t,
    snd_next, snd_prev, from_prev, from_next, bsnd_next, bsnd_prev, bfrom_prev, bfrom_next,
    rs_send, rs_rin, rs_fin, share, gp_buf, h_send, h_recv, h_keep,
    xs_send, xs_rin, xs_fin, z_send, z_recv, t_buf, f_recv,
    ssem, rsem,
):
    d = lax.axis_index("dp")
    t = lax.axis_index("tensor")
    xi = d // 16
    zi = lax.rem(d // 2, NZ)
    core = lax.rem(d, 2)
    inner = lax.rem(d, 16)
    t_right, t_left, t_far = lax.rem(t + 1, NT), lax.rem(t + 3, NT), lax.rem(t + 2, NT)
    x_right, x_left, x_far = lax.rem(xi + 1, NX), lax.rem(xi + 3, NX), lax.rem(xi + 2, NX)
    dp_next = (lax.rem(d + 1, 64), t)
    dp_prev = (lax.rem(d + 63, 64), t)
    mate = (d + 1 - 2 * core, t)
    y_right, y_left = (d, t_right), (d, t_left)
    px_right, px_left = (x_right * 16 + inner, t), (x_left * 16 + inner, t)
    z_peers = [
        (lax.rem(zi + k, NZ), (xi * 16 + lax.rem(zi + k, NZ) * 2 + core, t)) for k in range(1, NZ)
    ]
    n_low, go_full = acts.at[0], acts.at[1]

    barrier = pltpu.get_barrier_semaphore()
    greet = [dp_next, dp_prev, y_right, y_left, px_right, px_left] + [p for _, p in z_peers]
    for peer in greet:
        pl.semaphore_signal(barrier, inc=1, device_id=peer, device_id_type=MESH)

    counter = [0]
    pending = []

    def remote(src, dst, dev):
        k = counter[0]
        counter[0] += 1
        copy = pltpu.make_async_remote_copy(
            src_ref=src, dst_ref=dst, send_sem=ssem.at[k], recv_sem=rsem.at[k],
            device_id=dev, device_id_type=MESH,
        )
        copy.start()
        pending.append(copy)
        return copy

    lower = cut_ref[0, 0]
    upper = cut_ref[0, 1]
    head = jnp.maximum(lower, 0)
    tail = jnp.maximum(-upper, 0)

    r, c = grid2(SPILL, SRC)
    base = SEQ - lower + jnp.minimum(upper, 0)
    snd_next[...] = dot(hot(c == r + base), patches_ref[...], 1, 1).astype(BF)
    snd_prev[...] = dot(hot(c == r), patches_ref[...], 1, 1).astype(BF)

    pl.semaphore_wait(barrier, len(greet))

    to_next = remote(snd_next, from_prev, dp_next)
    to_prev = remote(snd_prev, from_next, dp_prev)

    half = COLS // 2
    lo, hi = pl.ds(0, half), pl.ds(half, half)

    def gather_start(src, full):
        ra = remote(src.at[lo], full.at[t, lo], y_right)
        lb = remote(src.at[hi], full.at[t, hi], y_left)
        rb = remote(src.at[hi], full.at[t, hi], y_right)
        la = remote(src.at[lo], full.at[t, lo], y_left)
        return ra, lb, rb, la

    def gather_relay(full, first):
        ra, lb, rb, la = first
        ra.wait_recv()
        fa = remote(full.at[t_left, lo], full.at[t_left, lo], y_right)
        lb.wait_recv()
        fb = remote(full.at[t_right, hi], full.at[t_right, hi], y_left)
        return rb, la, fa, fb

    def gather_finish(rest):
        for copy in rest:
            copy.wait_recv()

    go_first = gather_start(gout_ref, go_full)
    go_full[t] = gout_ref[...]

    r, c = grid2(SRC, SEQ)
    mine = (r == c - lower) & (c >= head) & (c < SEQ - tail)
    own = dot(patches_ref[...], hot(mine))
    r, c = grid2(SPILL, SEQ)
    pick_prev = hot((c == r) & (c < head))
    pick_next = hot((r == c - (SEQ - tail)) & (c >= SEQ - tail))
    to_next.wait_recv()
    to_prev.wait_recv()
    own = own + dot(from_prev[...], pick_prev, 0, 0) + dot(from_next[...], pick_next, 0, 0)
    x_full[t] = own.astype(BF)
    x_first = gather_start(x_full.at[t], x_full)
    go_rest = gather_relay(go_full, go_first)

    w_t[...] = jnp.transpose(wqkv_ref[...])
    wo_t[...] = jnp.transpose(wout_ref[...])

    x_rest = gather_relay(x_full, x_first)

    gather_finish(go_rest)
    grad_att = dot(wout_ref[...], go_full[...].reshape(MODEL, SEQ))

    gather_finish(x_rest)

    def rows_of(u):
        return x_full[u].astype(F32)

    mean = jnp.zeros((1, SEQ), F32)
    for u in range(NT):
        mean = mean + jnp.sum(rows_of(u), axis=0, keepdims=True)
    mean = mean * (1.0 / MODEL)
    spread = jnp.zeros((1, SEQ), F32)
    for u in range(NT):
        center = rows_of(u) - mean
        spread = spread + jnp.sum(center * center, axis=0, keepdims=True)
    rstd = lax.rsqrt(spread * (1.0 / MODEL) + norm_eps)
    for u in range(NT):
        n_low[u] = ((rows_of(u) - mean) * rstd).astype(BF)
    proj = dot(wqkv_ref[...], n_low[...].reshape(MODEL, SEQ))

    def head_norm(v):
        center = v - jnp.sum(v, axis=0, keepdims=True) * (1.0 / HD)
        var = jnp.sum(center * center, axis=0, keepdims=True) * (1.0 / HD)
        inverse = lax.rsqrt(var + norm_eps)
        return center * inverse, inverse

    def head_back(g, normed, inverse):
        first = jnp.sum(g, axis=0, keepdims=True) * (1.0 / HD)
        second = jnp.sum(g * normed, axis=0, keepdims=True) * (1.0 / HD)
        return inverse * (g - first - normed * second)

    seg_row = seg_ref[...].astype(F32)
    r, c = grid2(SEQ, SEQ)
    seg_col = jnp.sum(jnp.where(r == c, seg_row, 0.0), axis=-1, keepdims=True)
    same = seg_col == seg_row

    saved = []
    att_parts = []
    for h in range(2):
        q_hat, q_inv = head_norm(proj[h * HD : (h + 1) * HD])
        k_hat, k_inv = head_norm(proj[(2 + h) * HD : (3 + h) * HD])
        v = proj[(4 + h) * HD : (5 + h) * HD].astype(BF)
        q, k = q_hat.astype(BF), k_hat.astype(BF)
        raised = jnp.where(same, jnp.exp(dot(k, q, 0, 0) * score_scale), 0.0)
        weights = raised / jnp.sum(raised, axis=0, keepdims=True)
        weights_low = weights.astype(BF)
        att_parts.append(dot(v, weights_low))
        saved.append((q_hat, q_inv, k_hat, k_inv, q, k, v, weights, weights_low))
    att = jnp.concatenate(att_parts, axis=0).astype(BF)
    gp_buf[3] = att

    def scatter_start(send, rin, make, far, to_right, to_left, cut_at):
        a, b = pl.ds(0, cut_at), pl.ds(cut_at, cut_at)
        send[0] = make(far).astype(BF)
        ra = remote(send.at[0, a], rin.at[0], to_right)
        lb = remote(send.at[0, b], rin.at[1], to_left)
        return ra, lb

    def scatter_plain(send, fin, make, right, left, to_right, to_left, cut_at):
        a, b = pl.ds(0, cut_at), pl.ds(cut_at, cut_at)
        send[1] = make(right).astype(BF)
        rb = remote(send.at[1, b], fin.at[0, b], to_right)
        send[2] = make(left).astype(BF)
        la = remote(send.at[2, a], fin.at[1, a], to_left)
        return rb, la

    def scatter_relay(send, rin, fin, first, plain, to_right, to_left, cut_at):
        a, b = pl.ds(0, cut_at), pl.ds(cut_at, cut_at)
        ra, lb = first
        rb, la = plain
        ra.wait_recv()
        send[1, a] = (send[1, a].astype(F32) + rin[0].astype(F32)).astype(BF)
        fa = remote(send.at[1, a], fin.at[0, a], to_right)
        lb.wait_recv()
        send[2, b] = (send[2, b].astype(F32) + rin[1].astype(F32)).astype(BF)
        fb = remote(send.at[2, b], fin.at[1, b], to_left)
        return rb, la, fa, fb

    def branch(u):
        return dot(wo_t[pl.ds(pl.multiple_of(u * COLS, COLS), COLS), :], att)

    b_send, b_rin, b_fin = rs_send.at[0], rs_rin.at[0], rs_fin.at[0]
    b_first = scatter_start(b_send, b_rin, branch, t_far, y_right, y_left, half)
    b_plain = scatter_plain(b_send, b_fin, branch, t_right, t_left, y_right, y_left, half)
    mixed_own = x_full[t].astype(F32) + branch(t)

    grads = {}
    for h in range(2):
        q_hat, q_inv, k_hat, k_inv, q, k, v, weights, weights_low = saved[h]
        ga = grad_att[h * HD : (h + 1) * HD].astype(BF)
        gw = dot(v, ga, 0, 0)
        inner_sum = jnp.sum(gw * weights, axis=0, keepdims=True)
        gs = (weights * (gw - inner_sum) * score_scale).astype(BF)
        grads[0, h] = head_back(dot(k, gs), q_hat, q_inv)
        grads[1, h] = head_back(dot(q, gs, 1, 1), k_hat, k_inv)
        grads[2, h] = dot(ga, weights_low, 1, 1)
    for p in range(3):
        gp_buf[p] = jnp.concatenate([grads[p, 0], grads[p, 1]], axis=0).astype(BF)

    b_rest = scatter_relay(b_send, b_rin, b_fin, b_first, b_plain, y_right, y_left, half)

    order = [x_far, x_right, x_left, xi]

    def weight_grad(u, side):
        first = dot(n_low[u], gp_buf[2 * side], 1, 1)
        second = dot(acts[side, u], gp_buf[2 * side + 1], 1, 1)
        return jnp.concatenate([first, second], axis=1)

    h_copies = []
    for u in order:
        h_send[u] = weight_grad(u, 1 - core).astype(BF)
        h_copies.append(remote(h_send.at[u], h_recv.at[u], mate))

    gp = gp_buf[0:3].reshape(3 * QW, SEQ)
    s1 = jnp.zeros((1, SEQ), F32)
    s2 = jnp.zeros((1, SEQ), F32)
    for u in range(NT):
        part = dot(w_t[u * COLS : (u + 1) * COLS, :], gp)
        share[u] = part
        s1 = s1 + jnp.sum(part, axis=0, keepdims=True)
        s2 = s2 + jnp.sum(part * ((rows_of(u) - mean) * rstd), axis=0, keepdims=True)
    s1 = s1 * (1.0 / MODEL)
    s2 = s2 * (1.0 / MODEL)

    def back(u):
        return rstd * (share[u] - s1 - ((rows_of(u) - mean) * rstd) * s2)

    g_send, g_rin, g_fin = rs_send.at[1], rs_rin.at[1], rs_fin.at[1]
    g_first = scatter_start(g_send, g_rin, back, t_far, y_right, y_left, half)
    g_plain = scatter_plain(g_send, g_fin, back, t_right, t_left, y_right, y_left, half)

    for u in order:
        h_keep[u] = weight_grad(u, core)

    def pair(u):
        return h_keep[u] + h_recv[u].astype(F32)

    cut_x = COLS // 2
    h_copies[0].wait_recv()
    x_fst = scatter_start(xs_send, xs_rin, pair, x_far, px_right, px_left, cut_x)
    h_copies[1].wait_recv()
    h_copies[2].wait_recv()
    x_pln = scatter_plain(xs_send, xs_fin, pair, x_right, x_left, px_right, px_left, cut_x)

    gx_own = gout_ref[...].astype(F32) + back(t)

    for copy in b_rest:
        copy.wait_recv()
    mixed_ref[...] = (mixed_own + b_fin[0].astype(F32) + b_fin[1].astype(F32)).astype(BF)

    g_rest = scatter_relay(g_send, g_rin, g_fin, g_first, g_plain, y_right, y_left, half)
    x_rst = scatter_relay(xs_send, xs_rin, xs_fin, x_fst, x_pln, px_right, px_left, cut_x)
    h_copies[3].wait_recv()

    for copy in g_rest:
        copy.wait_recv()
    gx = (gx_own + g_fin[0].astype(F32) + g_fin[1].astype(F32)).astype(BF)
    r, c = grid2(SPILL, SEQ)
    bsnd_next[...] = dot(hot(c == r + SEQ - tail), gx, 1, 1).astype(BF)
    bsnd_prev[...] = dot(hot(c == r), gx, 1, 1).astype(BF)
    back_next = remote(bsnd_next, bfrom_prev, dp_next)
    back_prev = remote(bsnd_prev, bfrom_next, dp_prev)

    for copy in x_rst:
        copy.wait_recv()
    summed = (pair(xi) + xs_fin[0].astype(F32) + xs_fin[1].astype(F32)).astype(BF)
    block = 2 * CORE_ROWS
    for k in range(NZ):
        r, c = grid2(block, COLS)
        first = (r < SHARE) & (c == r + 2 * k * SHARE)
        second = (r >= CORE_ROWS) & (r < CORE_ROWS + SHARE)
        second = second & (c == r - CORE_ROWS + (2 * k + 1) * SHARE)
        z_send[k] = dot(hot(first | second), summed).astype(BF)
    z_copies = [remote(z_send.at[pz], z_recv.at[zi], dev) for pz, dev in z_peers]

    length = SEQ + upper - lower
    behind = jnp.maximum(-lower, 0)
    ahead = jnp.maximum(upper, 0)
    r, c = grid2(SEQ, SRC)
    mine = hot((r == c + lower) & (c >= behind) & (c < length - ahead))
    src_rows = dot(gx, mine)
    r, c = grid2(SPILL, SRC)
    pick_prev = hot((c == r) & (c < behind))
    pick_next = hot((r == c - (length - ahead)) & (c >= length - ahead) & (c < length))
    back_next.wait_recv()
    back_prev.wait_recv()
    src_rows = (
        src_rows + dot(bfrom_prev[...], pick_prev, 0, 0) + dot(bfrom_next[...], pick_next, 0, 0)
    )
    gpatch_ref[...] = src_rows.astype(BF)

    total = z_send[zi].astype(F32)
    for copy in z_copies:
        copy.wait_recv()
    for pz, _ in z_peers:
        total = total + z_recv[pz].astype(F32)
    total = total * total_scale
    t_buf[0] = total[0:CORE_ROWS]
    t_buf[1] = total[CORE_ROWS : 2 * CORE_ROWS]
    last = remote(t_buf.at[1 - core], f_recv, mate)
    kept = t_buf[core]
    last.wait_recv()
    got = f_recv[...]
    qk = jnp.where(core == 0, kept, got)
    vo = jnp.where(core == 0, got, kept)
    gqkv_ref[0] = qk[0:SHARE, 0:QW]
    gqkv_ref[1] = qk[0:SHARE, QW : 2 * QW]
    gqkv_ref[2] = vo[0:SHARE, 0:QW]
    gwout_ref[...] = vo[0:SHARE, QW : 2 * QW]

    for copy in pending:
        copy.wait_send()


COPIES = 48


def body(patches, seg_ids, cut, w_qkv, w_out, grad_out):
    vmem = pl.BlockSpec(memory_space=pltpu.VMEM)
    smem = pl.BlockSpec(memory_space=pltpu.SMEM)
    halo = pltpu.VMEM((SPILL, COLS), BF)
    scratch = [
        pltpu.VMEM((2, NT, COLS, SEQ), BF),
        pltpu.VMEM((NT, COLS, SEQ), BF),
        pltpu.VMEM((MODEL, 3 * QW), BF),
        pltpu.VMEM((MODEL, QW), BF),
        halo, halo, halo, halo, halo, halo, halo, halo,
        pltpu.VMEM((2, 3, COLS, SEQ), BF),
        pltpu.VMEM((2, 2, COLS // 2, SEQ), BF),
        pltpu.VMEM((2, 2, COLS, SEQ), BF),
        pltpu.VMEM((NT, COLS, SEQ), F32),
        pltpu.VMEM((4, QW, SEQ), BF),
        pltpu.VMEM((NT, COLS, COLS), BF),
        pltpu.VMEM((NT, COLS, COLS), BF),
        pltpu.VMEM((NT, COLS, COLS), F32),
        pltpu.VMEM((3, COLS, COLS), BF),
        pltpu.VMEM((2, COLS // 2, COLS), BF),
        pltpu.VMEM((2, COLS, COLS), BF),
        pltpu.VMEM((NZ, 2 * CORE_ROWS, COLS), BF),
        pltpu.VMEM((NZ, 2 * CORE_ROWS, COLS), BF),
        pltpu.VMEM((2, CORE_ROWS, COLS), F32),
        pltpu.VMEM((CORE_ROWS, COLS), F32),
        pltpu.SemaphoreType.DMA((COPIES,)),
        pltpu.SemaphoreType.DMA((COPIES,)),
    ]
    mixed, grad_patches, qkv_grad, out_grad = pl.pallas_call(
        kernel,
        out_shape=(
            jax.ShapeDtypeStruct((COLS, SEQ), BF),
            jax.ShapeDtypeStruct((COLS, SRC), BF),
            jax.ShapeDtypeStruct((3, SHARE, QW), F32),
            jax.ShapeDtypeStruct((SHARE, QW), F32),
        ),
        in_specs=[smem, vmem, vmem, vmem, vmem, vmem],
        out_specs=(vmem, vmem, vmem, vmem),
        scratch_shapes=scratch,
        compiler_params=pltpu.CompilerParams(
            collective_id=0, has_side_effects=True, vmem_limit_bytes=56 * 1024 * 1024
        ),
    )(cut, seg_ids.reshape(1, SEQ), patches.T, w_qkv.reshape(3 * QW, MODEL), w_out, grad_out.T)
    return mixed.T, grad_patches.T, jnp.swapaxes(qkv_grad, 1, 2), out_grad.T


def solution(mesh):
    in_specs = (
        P("dp", "tensor"),
        P("dp"),
        P("dp", None),
        P(None, "tensor", None),
        P("tensor", None),
        P("dp", "tensor"),
    )
    out_specs = (P("dp", "tensor"), P("dp", "tensor"), P(None, "tensor", "dp"), P("tensor", "dp"))
    return jax.shard_map(body, mesh=mesh, in_specs=in_specs, out_specs=out_specs, check_vma=False)
```

time: 70.4 us -> 63.5 us (0.902)
  local copies, waits for them, and re-layouts: 10.4 us -> 6.16 us
  Pallas kernels: 59.1 us -> 56.4 us
    pallas_call x4 -> x0, local copies, waits for them, and re-layouts: 6.88 us -> none  [body(): pl.pallas_call(kernel, out_shape=(jax.ShapeDtypeStruct((SEQ, COLS), BF),...]
    pallas_call x1, Pallas kernels: 59.1 us -> 56.4 us  [body(): pl.pallas_call(kernel, out_shape=(jax.ShapeDtypeStruct((COLS, SEQ), BF),...]
    unnamed x2 -> x4, local copies, waits for them, and re-layouts: 3.57 us -> 6.16 us
where the time goes in v2:
time: 63.5 us; the launch traced here: 63.2 us
  Pallas kernels  56.4 us (89%)
  local copies, waits for them, and re-layouts  6.16 us (10%)
  between operations  0.64 us (1%)
    pallas_call x1, Pallas kernels, body(): pl.pallas_call(kernel, out_shape=(jax.ShapeDtypeStruct((COLS, SEQ), BF),...  56.4 us
    unnamed x4, local copies, waits for them, and re-layouts  6.16 us

profile of v2, /device:TPU:1, one launch (start us, length us, event | category | flops | bytes accessed | tf_op | source)
XLA Modules:
  0.0 63.2 jit_solution(10469057734620500183)
XLA Ops:
  0.6 56.4 %shard_map.93 = (bf16[352,256]{1,0:T(8,128)(2,1)}, bf16[352,384]{1,0:T(8,128)(2,1)}, f32[3,22,176]{2,1,0:T(8,128)}, f32[22,176]{1,0:T(8,128)}) custom-call(s32[1,2]{1,0:T(1,128)} %cut_ref.1, s32[1,256]{1,0:T(1,128)} %bitcast.15, bf16[352,384]{1,0:T(8,128)(2,1)} %bitcast.9, bf16[528,1408]{1,0:T(8,128)(2,1)} %bitcast.8, bf16[176,1408]{1,0:T(8,128)(2,1)} %wout_ref.1, ...), custom_call_target="tpu_custom_call" | custom-call | tf_op jit(solution)/shard_map/pallas_call | solution.py:395
  57.1 1.6 %copy.14 = bf16[256,352]{0,1:T(8,128)(2,1)} copy(bf16[256,352]{0,1:T(8,128)(2,1)} %bitcast.11) | data formatting | bytes 360448
  58.7 1.7 %copy.15 = bf16[384,352]{0,1:T(8,128)(2,1)} copy(bf16[384,352]{0,1:T(8,128)(2,1)} %bitcast.10) | data formatting | bytes 540672
  60.4 1.5 %copy.16 = f32[3,176,22]{1,2,0:T(8,128)} copy(f32[3,176,22]{1,2,0:T(8,128)} %bitcast.13) | data formatting | bytes 92928
  61.9 1.3 %copy.17 = f32[176,22]{0,1:T(8,128)} copy(f32[176,22]{0,1:T(8,128)} %bitcast.14) | data formatting | bytes 30976

commit v3 on v2

--- a/solution.py
+++ b/solution.py
@@ -19,6 +19,7 @@
 NZ = 8
 SHARE = 22
 CORE_ROWS = 24
+KEPT = NZ * CORE_ROWS
 norm_eps = 1e-06
 score_scale = HD ** (-0.5)
 total_scale = 1.0 / math.sqrt(16384.0)
@@ -47,8 +48,8 @@
     mixed_ref, gpatch_ref, gqkv_ref, gwout_ref,
     acts, x_full, w_t, wo_t,
     snd_next, snd_prev, from_prev, from_next, bsnd_next, bsnd_prev, bfrom_prev, bfrom_next,
-    rs_send, rs_rin, rs_fin, share, gp_buf, h_send, h_recv, h_keep,
-    xs_send, xs_rin, xs_fin, z_send, z_recv, t_buf, f_recv,
+    rs_send, rs_rin, rs_fin, share, gp_buf, gp_mate, own_sel, out_sel, mate_sel,
+    xs_send, xs_rin, xs_fin, z_send, z_recv,
     ssem, rsem,
 ):
     d = lax.axis_index("dp")
@@ -139,16 +140,23 @@
     own = own + dot(from_prev[...], pick_prev, 0, 0) + dot(from_next[...], pick_next, 0, 0)
     x_full[t] = own.astype(BF)
     x_first = gather_start(x_full.at[t], x_full)
-    go_rest = gather_relay(go_full, go_first)
 
     w_t[...] = jnp.transpose(wqkv_ref[...])
     wo_t[...] = jnp.transpose(wout_ref[...])
 
+    r, c = grid2(KEPT, COLS)
+
+    def chosen(parity):
+        mask = c < 0
+        for k in range(NZ):
+            at = r - k * CORE_ROWS
+            mask = mask | ((at >= 0) & (at < SHARE) & (c == at + (2 * k + parity) * SHARE))
+        return hot(mask)
+
+    sel_own, sel_mate = chosen(core), chosen(1 - core)
+
     x_rest = gather_relay(x_full, x_first)
-
-    gather_finish(go_rest)
-    grad_att = dot(wout_ref[...], go_full[...].reshape(MODEL, SEQ))
-
+    go_rest = gather_relay(go_full, go_first)
     gather_finish(x_rest)
 
     def rows_of(u):
@@ -166,6 +174,16 @@
     for u in range(NT):
         n_low[u] = ((rows_of(u) - mean) * rstd).astype(BF)
     proj = dot(wqkv_ref[...], n_low[...].reshape(MODEL, SEQ))
+
+    def pick(kind):
+        for u in range(NT):
+            out_sel[kind, u] = dot(sel_mate, acts[kind, u]).astype(BF)
+        copy = remote(out_sel.at[kind], mate_sel.at[kind], mate)
+        for u in range(NT):
+            own_sel[kind, u] = dot(sel_own, acts[kind, u]).astype(BF)
+        return copy
+
+    n_copy = pick(0)
 
     def head_norm(v):
         center = v - jnp.sum(v, axis=0, keepdims=True) * (1.0 / HD)
@@ -197,8 +215,9 @@
         saved.append((q_hat, q_inv, k_hat, k_inv, q, k, v, weights, weights_low))
     att = jnp.concatenate(att_parts, axis=0).astype(BF)
     gp_buf[3] = att
-
-    def scatter_start(send, rin, make, far, to_right, to_left, cut_at):
+    att_copy = remote(gp_buf.at[3], gp_mate.at[3], mate)
+
+    def scatter_far(send, rin, make, far, to_right, to_left, cut_at):
         a, b = pl.ds(0, cut_at), pl.ds(cut_at, cut_at)
         send[0] = make(far).astype(BF)
         ra = remote(send.at[0, a], rin.at[0], to_right)
@@ -229,36 +248,49 @@
         return dot(wo_t[pl.ds(pl.multiple_of(u * COLS, COLS), COLS), :], att)
 
     b_send, b_rin, b_fin = rs_send.at[0], rs_rin.at[0], rs_fin.at[0]
-    b_first = scatter_start(b_send, b_rin, branch, t_far, y_right, y_left, half)
-    b_plain = scatter_plain(b_send, b_fin, branch, t_right, t_left, y_right, y_left, half)
-    mixed_own = x_full[t].astype(F32) + branch(t)
-
-    grads = {}
+    b_far = scatter_far(b_send, b_rin, branch, t_far, y_right, y_left, half)
+
+    gather_finish(go_rest)
+    grad_att = dot(wout_ref[...], go_full[...].reshape(MODEL, SEQ))
+    gas = [grad_att[h * HD : (h + 1) * HD].astype(BF) for h in range(2)]
+    gvs = [dot(gas[h], saved[h][8], 1, 1) for h in range(2)]
+    gp_buf[2] = jnp.concatenate(gvs, axis=0).astype(BF)
+    v_copy = remote(gp_buf.at[2], gp_mate.at[2], mate)
+    go_copy = pick(1)
+
+    gqs, gks = [], []
     for h in range(2):
         q_hat, q_inv, k_hat, k_inv, q, k, v, weights, weights_low = saved[h]
-        ga = grad_att[h * HD : (h + 1) * HD].astype(BF)
-        gw = dot(v, ga, 0, 0)
+        gw = dot(v, gas[h], 0, 0)
         inner_sum = jnp.sum(gw * weights, axis=0, keepdims=True)
         gs = (weights * (gw - inner_sum) * score_scale).astype(BF)
-        grads[0, h] = head_back(dot(k, gs), q_hat, q_inv)
-        grads[1, h] = head_back(dot(q, gs, 1, 1), k_hat, k_inv)
-        grads[2, h] = dot(ga, weights_low, 1, 1)
-    for p in range(3):
-        gp_buf[p] = jnp.concatenate([grads[p, 0], grads[p, 1]], axis=0).astype(BF)
-
-    b_rest = scatter_relay(b_send, b_rin, b_fin, b_first, b_plain, y_right, y_left, half)
-
-    order = [x_far, x_right, x_left, xi]
-
-    def weight_grad(u, side):
-        first = dot(n_low[u], gp_buf[2 * side], 1, 1)
-        second = dot(acts[side, u], gp_buf[2 * side + 1], 1, 1)
+        gqs.append(head_back(dot(k, gs), q_hat, q_inv))
+        gks.append(head_back(dot(q, gs, 1, 1), k_hat, k_inv))
+    gp_buf[0] = jnp.concatenate(gqs, axis=0).astype(BF)
+    gp_buf[1] = jnp.concatenate(gks, axis=0).astype(BF)
+    qk_copy = remote(gp_buf.at[pl.ds(0, 2)], gp_mate.at[pl.ds(0, 2)], mate)
+
+    def grad_vo(u):
+        first = dot(own_sel[0, u], gp_buf[2], 1, 1) + dot(mate_sel[0, u], gp_mate[2], 1, 1)
+        second = dot(own_sel[1, u], gp_buf[3], 1, 1) + dot(mate_sel[1, u], gp_mate[3], 1, 1)
         return jnp.concatenate([first, second], axis=1)
 
-    h_copies = []
-    for u in order:
-        h_send[u] = weight_grad(u, 1 - core).astype(BF)
-        h_copies.append(remote(h_send.at[u], h_recv.at[u], mate))
+    def grad_qk(u):
+        ours = gp_buf[0:2].reshape(2 * QW, SEQ)
+        theirs = gp_mate[0:2].reshape(2 * QW, SEQ)
+        return dot(own_sel[0, u], ours, 1, 1) + dot(mate_sel[0, u], theirs, 1, 1)
+
+    cut_x = KEPT // 2
+    n_copy.wait_recv()
+    att_copy.wait_recv()
+    v_copy.wait_recv()
+    go_copy.wait_recv()
+    v_send, v_rin, v_fin = xs_send.at[0], xs_rin.at[0], xs_fin.at[0]
+    q_send, q_rin, q_fin = xs_send.at[1], xs_rin.at[1], xs_fin.at[1]
+    v_far = scatter_far(v_send, v_rin, grad_vo, x_far, px_right, px_left, cut_x)
+    v_plain = scatter_plain(
+        v_send, v_fin, grad_vo, x_right, x_left, px_right, px_left, cut_x
+    )
 
     gp = gp_buf[0:3].reshape(3 * QW, SEQ)
     s1 = jnp.zeros((1, SEQ), F32)
@@ -275,31 +307,24 @@
         return rstd * (share[u] - s1 - ((rows_of(u) - mean) * rstd) * s2)
 
     g_send, g_rin, g_fin = rs_send.at[1], rs_rin.at[1], rs_fin.at[1]
-    g_first = scatter_start(g_send, g_rin, back, t_far, y_right, y_left, half)
+    g_far = scatter_far(g_send, g_rin, back, t_far, y_right, y_left, half)
     g_plain = scatter_plain(g_send, g_fin, back, t_right, t_left, y_right, y_left, half)
 
-    for u in order:
-        h_keep[u] = weight_grad(u, core)
-
-    def pair(u):
-        return h_keep[u] + h_recv[u].astype(F32)
-
-    cut_x = COLS // 2
-    h_copies[0].wait_recv()
-    x_fst = scatter_start(xs_send, xs_rin, pair, x_far, px_right, px_left, cut_x)
-    h_copies[1].wait_recv()
-    h_copies[2].wait_recv()
-    x_pln = scatter_plain(xs_send, xs_fin, pair, x_right, x_left, px_right, px_left, cut_x)
-
+    qk_copy.wait_recv()
+    q_far = scatter_far(q_send, q_rin, grad_qk, x_far, px_right, px_left, cut_x)
+    q_plain = scatter_plain(
+        q_send, q_fin, grad_qk, x_right, x_left, px_right, px_left, cut_x
+    )
+    v_rest = scatter_relay(v_send, v_rin, v_fin, v_far, v_plain, px_right, px_left, cut_x)
+    g_rest = scatter_relay(g_send, g_rin, g_fin, g_far, g_plain, y_right, y_left, half)
+    q_rest = scatter_relay(q_send, q_rin, q_fin, q_far, q_plain, px_right, px_left, cut_x)
+    b_plain = scatter_plain(b_send, b_fin, branch, t_right, t_left, y_right, y_left, half)
+    b_rest = scatter_relay(b_send, b_rin, b_fin, b_far, b_plain, y_right, y_left, half)
+
+    mixed_own = x_full[t].astype(F32) + branch(t)
     gx_own = gout_ref[...].astype(F32) + back(t)
-
-    for copy in b_rest:
-        copy.wait_recv()
-    mixed_ref[...] = (mixed_own + b_fin[0].astype(F32) + b_fin[1].astype(F32)).astype(BF)
-
-    g_rest = scatter_relay(g_send, g_rin, g_fin, g_first, g_plain, y_right, y_left, half)
-    x_rst = scatter_relay(xs_send, xs_rin, xs_fin, x_fst, x_pln, px_right, px_left, cut_x)
-    h_copies[3].wait_recv()
+    v_own = grad_vo(xi)
+    q_own = grad_qk(xi)
 
     for copy in g_rest:
         copy.wait_recv()
@@ -310,16 +335,15 @@
     back_next = remote(bsnd_next, bfrom_prev, dp_next)
     back_prev = remote(bsnd_prev, bfrom_next, dp_prev)
 
-    for copy in x_rst:
+    for copy in v_rest:
         copy.wait_recv()
-    summed = (pair(xi) + xs_fin[0].astype(F32) + xs_fin[1].astype(F32)).astype(BF)
-    block = 2 * CORE_ROWS
+    v_sum = v_own + v_fin[0].astype(F32) + v_fin[1].astype(F32)
+    for copy in q_rest:
+        copy.wait_recv()
+    q_sum = q_own + q_fin[0].astype(F32) + q_fin[1].astype(F32)
     for k in range(NZ):
-        r, c = grid2(block, COLS)
-        first = (r < SHARE) & (c == r + 2 * k * SHARE)
-        second = (r >= CORE_ROWS) & (r < CORE_ROWS + SHARE)
-        second = second & (c == r - CORE_ROWS + (2 * k + 1) * SHARE)
-        z_send[k] = dot(hot(first | second), summed).astype(BF)
+        at = slice(k * CORE_ROWS, (k + 1) * CORE_ROWS)
+        z_send[k] = jnp.concatenate([q_sum[at], v_sum[at]], axis=0).astype(BF)
     z_copies = [remote(z_send.at[pz], z_recv.at[zi], dev) for pz, dev in z_peers]
 
     length = SEQ + upper - lower
@@ -338,35 +362,43 @@
     )
     gpatch_ref[...] = src_rows.astype(BF)
 
+    for copy in b_rest:
+        copy.wait_recv()
+    mixed_ref[...] = (mixed_own + b_fin[0].astype(F32) + b_fin[1].astype(F32)).astype(BF)
+
     total = z_send[zi].astype(F32)
     for copy in z_copies:
         copy.wait_recv()
     for pz, _ in z_peers:
         total = total + z_recv[pz].astype(F32)
     total = total * total_scale
-    t_buf[0] = total[0:CORE_ROWS]
-    t_buf[1] = total[CORE_ROWS : 2 * CORE_ROWS]
-    last = remote(t_buf.at[1 - core], f_recv, mate)
-    kept = t_buf[core]
-    last.wait_recv()
-    got = f_recv[...]
-    qk = jnp.where(core == 0, kept, got)
-    vo = jnp.where(core == 0, got, kept)
-    gqkv_ref[0] = qk[0:SHARE, 0:QW]
-    gqkv_ref[1] = qk[0:SHARE, QW : 2 * QW]
-    gqkv_ref[2] = vo[0:SHARE, 0:QW]
-    gwout_ref[...] = vo[0:SHARE, QW : 2 * QW]
+    gqkv_ref[0] = total[0:SHARE, 0:QW]
+    gqkv_ref[1] = total[0:SHARE, QW : 2 * QW]
+    gqkv_ref[2] = total[CORE_ROWS : CORE_ROWS + SHARE, 0:QW]
+    gwout_ref[...] = total[CORE_ROWS : CORE_ROWS + SHARE, QW : 2 * QW]
 
     for copy in pending:
         copy.wait_send()
 
 
-COPIES = 48
+def hand_out(a, b, c, e, a_out, b_out, c_out, e_out, sems):
+    pairs = [(a, a_out), (b, b_out), (c, c_out), (e, e_out)]
+    copies = [
+        pltpu.make_async_copy(src, dst, sems.at[k]) for k, (src, dst) in enumerate(pairs)
+    ]
+    for copy in copies:
+        copy.start()
+    for copy in copies:
+        copy.wait()
+
+
+COPIES = 56
 
 
 def body(patches, seg_ids, cut, w_qkv, w_out, grad_out):
     vmem = pl.BlockSpec(memory_space=pltpu.VMEM)
     smem = pl.BlockSpec(memory_space=pltpu.SMEM)
+    anym = pl.BlockSpec(memory_space=pl.ANY)
     halo = pltpu.VMEM((SPILL, COLS), BF)
     scratch = [
         pltpu.VMEM((2, NT, COLS, SEQ), BF),
@@ -379,27 +411,27 @@
         pltpu.VMEM((2, 2, COLS, SEQ), BF),
         pltpu.VMEM((NT, COLS, SEQ), F32),
         pltpu.VMEM((4, QW, SEQ), BF),
-        pltpu.VMEM((NT, COLS, COLS), BF),
-        pltpu.VMEM((NT, COLS, COLS), BF),
-        pltpu.VMEM((NT, COLS, COLS), F32),
-        pltpu.VMEM((3, COLS, COLS), BF),
-        pltpu.VMEM((2, COLS // 2, COLS), BF),
-        pltpu.VMEM((2, COLS, COLS), BF),
+        pltpu.VMEM((4, QW, SEQ), BF),
+        pltpu.VMEM((2, NX, KEPT, SEQ), BF),
+        pltpu.VMEM((2, NX, KEPT, SEQ), BF),
+        pltpu.VMEM((2, NX, KEPT, SEQ), BF),
+        pltpu.VMEM((2, 3, KEPT, COLS), BF),
+        pltpu.VMEM((2, 2, KEPT // 2, COLS), BF),
+        pltpu.VMEM((2, 2, KEPT, COLS), BF),
         pltpu.VMEM((NZ, 2 * CORE_ROWS, COLS), BF),
         pltpu.VMEM((NZ, 2 * CORE_ROWS, COLS), BF),
-        pltpu.VMEM((2, CORE_ROWS, COLS), F32),
-        pltpu.VMEM((CORE_ROWS, COLS), F32),
         pltpu.SemaphoreType.DMA((COPIES,)),
         pltpu.SemaphoreType.DMA((COPIES,)),
     ]
-    mixed, grad_patches, qkv_grad, out_grad = pl.pallas_call(
+    out_shape = (
+        jax.ShapeDtypeStruct((COLS, SEQ), BF),
+        jax.ShapeDtypeStruct((COLS, SRC), BF),
+        jax.ShapeDtypeStruct((3, SHARE, QW), F32),
+        jax.ShapeDtypeStruct((SHARE, QW), F32),
+    )
+    results = pl.pallas_call(
         kernel,
-        out_shape=(
-            jax.ShapeDtypeStruct((COLS, SEQ), BF),
-            jax.ShapeDtypeStruct((COLS, SRC), BF),
-            jax.ShapeDtypeStruct((3, SHARE, QW), F32),
-            jax.ShapeDtypeStruct((SHARE, QW), F32),
-        ),
+        out_shape=out_shape,
         in_specs=[smem, vmem, vmem, vmem, vmem, vmem],
         out_specs=(vmem, vmem, vmem, vmem),
         scratch_shapes=scratch,
@@ -407,6 +439,13 @@
             collective_id=0, has_side_effects=True, vmem_limit_bytes=56 * 1024 * 1024
         ),
     )(cut, seg_ids.reshape(1, SEQ), patches.T, w_qkv.reshape(3 * QW, MODEL), w_out, grad_out.T)
+    mixed, grad_patches, qkv_grad, out_grad = pl.pallas_call(
+        hand_out,
+        out_shape=out_shape,
+        in_specs=[anym, anym, anym, anym],
+        out_specs=(anym, anym, anym, anym),
+        scratch_shapes=[pltpu.SemaphoreType.DMA((4,))],
+    )(*results)
     return mixed.T, grad_patches.T, jnp.swapaxes(qkv_grad, 1, 2), out_grad.T
 
 

time: 63.5 us -> 69.7 us (1.098)
  Pallas kernels: 56.4 us -> 68.9 us
  local copies, waits for them, and re-layouts: 6.16 us -> 0 us
    pallas_call x1 -> x2, Pallas kernels: 56.4 us -> 68.9 us  [the longest x1 51.2 us: body(): pl.pallas_call(kernel, out_shape=out_shape, in_specs=[smem, vmem, vmem, v...]
    unnamed x4 -> x0, local copies, waits for them, and re-layouts: 6.16 us -> none
where the time goes in v3:
time: 69.7 us; the launch traced here: 69.6 us
  Pallas kernels  68.9 us (99%)
    pallas_call x1, Pallas kernels, body(): pl.pallas_call(kernel, out_shape=out_shape, in_specs=[smem, vmem, vmem, v...  51.2 us
    pallas_call x1, Pallas kernels, body(): pl.pallas_call(hand_out, out_shape=out_shape, in_specs=[anym, anym, anym,...  17.8 us

profile of v3, /device:TPU:1, one launch (start us, length us, event | category | flops | bytes accessed | tf_op | source)
XLA Modules:
  0.0 69.6 jit_solution(17823918191229637274)
XLA Ops:
  0.6 51.2 %shard_map.93 = (bf16[352,256]{1,0:T(8,128)(2,1)}, bf16[352,384]{1,0:T(8,128)(2,1)}, f32[3,22,176]{2,1,0:T(8,128)}, f32[22,176]{1,0:T(8,128)}) custom-call(s32[1,2]{1,0:T(1,128)} %cut_ref.1, s32[1,256]{1,0:T(1,128)} %bitcast.11, bf16[352,384]{1,0:T(8,128)(2,1)} %bitcast.9, bf16[528,1408]{1,0:T(8,128)(2,1)} %bitcast.8, bf16[176,1408]{1,0:T(8,128)(2,1)} %wout_ref.1, ...), custom_call_target="tpu_custom_call" | custom-call | tf_op jit(solution)/shard_map/pallas_call | solution.py:432
  51.8 17.8 %shard_map.94 = (bf16[352,256]{1,0:T(8,128)(2,1)}, bf16[352,384]{1,0:T(8,128)(2,1)}, f32[3,22,176]{2,1,0:T(8,128)}, f32[22,176]{1,0:T(8,128)}) custom-call(bf16[352,256]{1,0:T(8,128)(2,1)} %get-tuple-element.12.a, bf16[352,384]{1,0:T(8,128)(2,1)} %get-tuple-element.13.b, f32[3,22,176]{2,1,0:T(8,128)} %get-tuple-element.14.c, f32[22,176]{1,0:T(8,128)} %get-tuple-element.15.e), custom_call_target="tpu_custom_call" | custom-call | tf_op jit(solution)/shard_map/pallas_call | solution.py:442

commit v4 on v3

--- a/solution.py
+++ b/solution.py
@@ -381,15 +381,11 @@
         copy.wait_send()
 
 
-def hand_out(a, b, c, e, a_out, b_out, c_out, e_out, sems):
-    pairs = [(a, a_out), (b, b_out), (c, c_out), (e, e_out)]
-    copies = [
-        pltpu.make_async_copy(src, dst, sems.at[k]) for k, (src, dst) in enumerate(pairs)
-    ]
-    for copy in copies:
-        copy.start()
-    for copy in copies:
-        copy.wait()
+def hand_out(a, b, c, e, a_out, b_out, c_out, e_out):
+    a_out[...] = a[...]
+    b_out[...] = b[...]
+    c_out[...] = c[...]
+    e_out[...] = e[...]
 
 
 COPIES = 56
@@ -398,7 +394,6 @@
 def body(patches, seg_ids, cut, w_qkv, w_out, grad_out):
     vmem = pl.BlockSpec(memory_space=pltpu.VMEM)
     smem = pl.BlockSpec(memory_space=pltpu.SMEM)
-    anym = pl.BlockSpec(memory_space=pl.ANY)
     halo = pltpu.VMEM((SPILL, COLS), BF)
     scratch = [
         pltpu.VMEM((2, NT, COLS, SEQ), BF),
@@ -442,9 +437,8 @@
     mixed, grad_patches, qkv_grad, out_grad = pl.pallas_call(
         hand_out,
         out_shape=out_shape,
-        in_specs=[anym, anym, anym, anym],
-        out_specs=(anym, anym, anym, anym),
-        scratch_shapes=[pltpu.SemaphoreType.DMA((4,))],
+        in_specs=[vmem, vmem, vmem, vmem],
+        out_specs=(vmem, vmem, vmem, vmem),
     )(*results)
     return mixed.T, grad_patches.T, jnp.swapaxes(qkv_grad, 1, 2), out_grad.T
 

time: 69.7 us -> 53.8 us (0.77)
  Pallas kernels: 68.9 us -> 53 us
    pallas_call x1, Pallas kernels: 17.8 us -> 1.86 us  [body(): pl.pallas_call(hand_out, out_shape=out_shape, in_specs=[vmem, vmem, vmem,...]
where the time goes in v4:
time: 53.8 us; the launch traced here: 53.7 us
  Pallas kernels  53 us (99%)
  between operations  0.64 us (1%)
    pallas_call x1, Pallas kernels, body(): pl.pallas_call(kernel, out_shape=out_shape, in_specs=[smem, vmem, vmem, v...  51.2 us
    pallas_call x1, Pallas kernels, body(): pl.pallas_call(hand_out, out_shape=out_shape, in_specs=[vmem, vmem, vmem,...  1.86 us

profile of v4, /device:TPU:1, one launch (start us, length us, event | category | flops | bytes accessed | tf_op | source)
XLA Modules:
  0.0 53.7 jit_solution(3062243664246769508)
XLA Ops:
  0.6 51.2 %shard_map.93 = (bf16[352,256]{1,0:T(8,128)(2,1)}, bf16[352,384]{1,0:T(8,128)(2,1)}, f32[3,22,176]{2,1,0:T(8,128)}, f32[22,176]{1,0:T(8,128)}) custom-call(s32[1,2]{1,0:T(1,128)} %cut_ref.1, s32[1,256]{1,0:T(1,128)} %bitcast.11, bf16[352,384]{1,0:T(8,128)(2,1)} %bitcast.9, bf16[528,1408]{1,0:T(8,128)(2,1)} %bitcast.8, bf16[176,1408]{1,0:T(8,128)(2,1)} %wout_ref.1, ...), custom_call_target="tpu_custom_call" | custom-call | tf_op jit(solution)/shard_map/pallas_call | solution.py:427
  51.8 1.9 %shard_map.94 = (bf16[352,256]{1,0:T(8,128)(2,1)}, bf16[352,384]{1,0:T(8,128)(2,1)}, f32[3,22,176]{2,1,0:T(8,128)}, f32[22,176]{1,0:T(8,128)}) custom-call(bf16[352,256]{1,0:T(8,128)(2,1)} %get-tuple-element.12.a, bf16[352,384]{1,0:T(8,128)(2,1)} %get-tuple-element.13.b, f32[3,22,176]{2,1,0:T(8,128)} %get-tuple-element.14.c, f32[22,176]{1,0:T(8,128)} %get-tuple-element.15.e), custom_call_target="tpu_custom_call" | custom-call | tf_op jit(solution)/shard_map/pallas_call | solution.py:437

commit v5 on v4

--- a/solution.py
+++ b/solution.py
@@ -18,8 +18,10 @@
 NX = 4
 NZ = 8
 SHARE = 22
-CORE_ROWS = 24
-KEPT = NZ * CORE_ROWS
+XROWS = 16
+ZROWS = SHARE - XROWS
+KEPT = NZ * XROWS
+REST = NX * ZROWS
 norm_eps = 1e-06
 score_scale = HD ** (-0.5)
 total_scale = 1.0 / math.sqrt(16384.0)
@@ -44,13 +46,14 @@
 
 
 def kernel(
-    cut_ref, seg_ref, patches_ref, wqkv_ref, wout_ref, gout_ref,
+    cut_ref, seg_ref, patches_in, wqkv_in, wout_in, gout_in,
     mixed_ref, gpatch_ref, gqkv_ref, gwout_ref,
-    acts, x_full, w_t, wo_t,
+    patches_ref, wqkv_ref, wout_ref, acts, x_full, w_t, wo_t,
     snd_next, snd_prev, from_prev, from_next, bsnd_next, bsnd_prev, bfrom_prev, bfrom_next,
     rs_send, rs_rin, rs_fin, share, gp_buf, gp_mate, own_sel, out_sel, mate_sel,
-    xs_send, xs_rin, xs_fin, z_send, z_recv,
-    ssem, rsem,
+    z_pick, own_rest, out_rest, mate_rest,
+    xs_send, xs_rin, xs_fin, z_send, z_recv, rz_send, rz_recv, rx_send, rx_recv,
+    ssem, rsem, lsem,
 ):
     d = lax.axis_index("dp")
     t = lax.axis_index("tensor")
@@ -66,12 +69,28 @@
     y_right, y_left = (d, t_right), (d, t_left)
     px_right, px_left = (x_right * 16 + inner, t), (x_left * 16 + inner, t)
     z_peers = [
-        (lax.rem(zi + k, NZ), (xi * 16 + lax.rem(zi + k, NZ) * 2 + core, t)) for k in range(1, NZ)
+        (lax.rem(zi + k, NZ), (xi * 16 + lax.rem(zi + k, NZ) * 2 + core, t)) for k in (4, 3, 5, 2, 6, 1, 7)
     ]
     n_low, go_full = acts.at[0], acts.at[1]
 
+    loads = [
+        pltpu.make_async_copy(src, dst, lsem.at[k])
+        for k, (src, dst) in enumerate(
+            [
+                (patches_in, patches_ref),
+                (gout_in, go_full.at[t]),
+                (wqkv_in, wqkv_ref),
+                (wout_in, wout_ref),
+            ]
+        )
+    ]
+    for load in loads:
+        load.start()
+
     barrier = pltpu.get_barrier_semaphore()
-    greet = [dp_next, dp_prev, y_right, y_left, px_right, px_left] + [p for _, p in z_peers]
+    px_far = (x_far * 16 + inner, t)
+    greet = [dp_next, dp_prev, y_right, y_left, px_right, px_left, px_far]
+    greet = greet + [p for _, p in z_peers]
     for peer in greet:
         pl.semaphore_signal(barrier, inc=1, device_id=peer, device_id_type=MESH)
 
@@ -94,6 +113,7 @@
     head = jnp.maximum(lower, 0)
     tail = jnp.maximum(-upper, 0)
 
+    loads[0].wait()
     r, c = grid2(SPILL, SRC)
     base = SEQ - lower + jnp.minimum(upper, 0)
     snd_next[...] = dot(hot(c == r + base), patches_ref[...], 1, 1).astype(BF)
@@ -107,27 +127,37 @@
     half = COLS // 2
     lo, hi = pl.ds(0, half), pl.ds(half, half)
 
-    def gather_start(src, full):
-        ra = remote(src.at[lo], full.at[t, lo], y_right)
-        lb = remote(src.at[hi], full.at[t, hi], y_left)
-        rb = remote(src.at[hi], full.at[t, hi], y_right)
-        la = remote(src.at[lo], full.at[t, lo], y_left)
-        return ra, lb, rb, la
-
-    def gather_relay(full, first):
-        ra, lb, rb, la = first
-        ra.wait_recv()
-        fa = remote(full.at[t_left, lo], full.at[t_left, lo], y_right)
-        lb.wait_recv()
-        fb = remote(full.at[t_right, hi], full.at[t_right, hi], y_left)
-        return rb, la, fa, fb
+    lo_pieces = pl.ds(0, 96), pl.ds(96, 80)
+    hi_pieces = pl.ds(half, 96), pl.ds(half + 96, 80)
+
+    def gather_handed(full):
+        handed = []
+        for low, high in zip(lo_pieces, hi_pieces):
+            handed.append(remote(full.at[t, low], full.at[t, low], y_right))
+            handed.append(remote(full.at[t, high], full.at[t, high], y_left))
+        return handed
+
+    def gather_other(full):
+        rb = remote(full.at[t, hi], full.at[t, hi], y_right)
+        la = remote(full.at[t, lo], full.at[t, lo], y_left)
+        return [rb, la]
+
+    def gather_relay(full, handed):
+        rest = []
+        for k, (low, high) in enumerate(zip(lo_pieces, hi_pieces)):
+            handed[2 * k].wait_recv()
+            rest.append(remote(full.at[t_left, low], full.at[t_left, low], y_right))
+            handed[2 * k + 1].wait_recv()
+            rest.append(remote(full.at[t_right, high], full.at[t_right, high], y_left))
+        return rest
 
     def gather_finish(rest):
         for copy in rest:
             copy.wait_recv()
 
-    go_first = gather_start(gout_ref, go_full)
-    go_full[t] = gout_ref[...]
+    loads[1].wait()
+    go_handed = gather_handed(go_full)
+    go_other = gather_other(go_full)
 
     r, c = grid2(SRC, SEQ)
     mine = (r == c - lower) & (c >= head) & (c < SEQ - tail)
@@ -135,55 +165,78 @@
     r, c = grid2(SPILL, SEQ)
     pick_prev = hot((c == r) & (c < head))
     pick_next = hot((r == c - (SEQ - tail)) & (c >= SEQ - tail))
+    loads[2].wait()
+    loads[3].wait()
+    w_t[...] = jnp.transpose(wqkv_ref[...])
+    wo_t[...] = jnp.transpose(wout_ref[...])
+
     to_next.wait_recv()
     to_prev.wait_recv()
     own = own + dot(from_prev[...], pick_prev, 0, 0) + dot(from_next[...], pick_next, 0, 0)
     x_full[t] = own.astype(BF)
-    x_first = gather_start(x_full.at[t], x_full)
-
-    w_t[...] = jnp.transpose(wqkv_ref[...])
-    wo_t[...] = jnp.transpose(wout_ref[...])
-
-    r, c = grid2(KEPT, COLS)
-
-    def chosen(parity):
-        mask = c < 0
-        for k in range(NZ):
-            at = r - k * CORE_ROWS
-            mask = mask | ((at >= 0) & (at < SHARE) & (c == at + (2 * k + parity) * SHARE))
-        return hot(mask)
-
-    sel_own, sel_mate = chosen(core), chosen(1 - core)
-
-    x_rest = gather_relay(x_full, x_first)
-    go_rest = gather_relay(go_full, go_first)
-    gather_finish(x_rest)
+    x_handed = gather_handed(x_full)
+    x_other = gather_other(x_full)
+    go_rest = gather_relay(go_full, go_handed)
+
+    r = lax.broadcasted_iota(jnp.int32, (KEPT, 1), 0)
+    zk = sum((r >= k * XROWS).astype(jnp.int32) for k in range(1, NZ))
+    at_x = r - zk * XROWS + 2 * SHARE * zk
+    _, c = grid2(KEPT, COLS)
+    x_own, x_mate = (hot(c == at_x + SHARE * side) for side in (core, 1 - core))
+    r = lax.broadcasted_iota(jnp.int32, (NZ * REST, 1), 0)
+    zk = sum((r >= k * REST).astype(jnp.int32) for k in range(1, NZ))
+    r = r - zk * REST
+    xk = sum((r >= k * ZROWS).astype(jnp.int32) for k in range(1, NX))
+    at_z = r - xk * ZROWS + COLS * xk + 2 * SHARE * zk + XROWS
+    _, c = grid2(NZ * REST, MODEL)
+    z_pick[0] = hot(c == at_z + SHARE * core)
+    z_pick[1] = hot(c == at_z + SHARE * (1 - core))
+
+    def pick_rest(kind):
+        everything = acts[kind].reshape(MODEL, SEQ)
+        out_rest[kind] = dot(z_pick[1], everything).astype(BF)
+        copy = remote(out_rest.at[kind], mate_rest.at[kind], mate)
+        own_rest[kind] = dot(z_pick[0], everything).astype(BF)
+        return copy
+
+    def pick(kind, u):
+        out_sel[kind, u] = dot(x_mate, acts[kind, u]).astype(BF)
+        return remote(out_sel.at[kind, u], mate_sel.at[kind, u], mate)
+
+    def pick_own(kind, u):
+        own_sel[kind, u] = dot(x_own, acts[kind, u]).astype(BF)
 
     def rows_of(u):
         return x_full[u].astype(F32)
 
-    mean = jnp.zeros((1, SEQ), F32)
-    for u in range(NT):
-        mean = mean + jnp.sum(rows_of(u), axis=0, keepdims=True)
-    mean = mean * (1.0 / MODEL)
+    def chunk_stats(u):
+        rows = rows_of(u)
+        centre = jnp.sum(rows, axis=0, keepdims=True) * (1.0 / COLS)
+        rows = rows - centre
+        return centre, jnp.sum(rows * rows, axis=0, keepdims=True)
+
+    x_rest = gather_relay(x_full, x_handed)
+    gather_finish(go_other)
+    go_copies = [pick(1, u) for u in (t, t_left, t_right)]
+    gather_finish(x_other)
+    stats = [chunk_stats(u) for u in (t, t_left, t_right)]
+    gather_finish(go_rest)
+    go_copies.append(pick(1, t_far))
+    go_copies.append(pick_rest(1))
+    grad_att = dot(wout_ref[...], go_full[...].reshape(MODEL, SEQ))
+    gas = [grad_att[h * HD : (h + 1) * HD].astype(BF) for h in range(2)]
+    gather_finish(x_rest)
+    stats.append(chunk_stats(t_far))
+
+    mean = (stats[0][0] + stats[1][0] + stats[2][0] + stats[3][0]) * (1.0 / NT)
     spread = jnp.zeros((1, SEQ), F32)
-    for u in range(NT):
-        center = rows_of(u) - mean
-        spread = spread + jnp.sum(center * center, axis=0, keepdims=True)
+    for centre, squares in stats:
+        spread = spread + squares + COLS * (centre - mean) * (centre - mean)
     rstd = lax.rsqrt(spread * (1.0 / MODEL) + norm_eps)
     for u in range(NT):
         n_low[u] = ((rows_of(u) - mean) * rstd).astype(BF)
     proj = dot(wqkv_ref[...], n_low[...].reshape(MODEL, SEQ))
-
-    def pick(kind):
-        for u in range(NT):
-            out_sel[kind, u] = dot(sel_mate, acts[kind, u]).astype(BF)
-        copy = remote(out_sel.at[kind], mate_sel.at[kind], mate)
-        for u in range(NT):
-            own_sel[kind, u] = dot(sel_own, acts[kind, u]).astype(BF)
-        return copy
-
-    n_copy = pick(0)
+    n_copies = [pick(0, u) for u in range(NT)] + [pick_rest(0)]
 
     def head_norm(v):
         center = v - jnp.sum(v, axis=0, keepdims=True) * (1.0 / HD)
@@ -218,14 +271,14 @@
     att_copy = remote(gp_buf.at[3], gp_mate.at[3], mate)
 
     def scatter_far(send, rin, make, far, to_right, to_left, cut_at):
-        a, b = pl.ds(0, cut_at), pl.ds(cut_at, cut_at)
+        a, b = cut_at
         send[0] = make(far).astype(BF)
-        ra = remote(send.at[0, a], rin.at[0], to_right)
-        lb = remote(send.at[0, b], rin.at[1], to_left)
+        ra = remote(send.at[0, a], rin.at[a], to_right)
+        lb = remote(send.at[0, b], rin.at[b], to_left)
         return ra, lb
 
     def scatter_plain(send, fin, make, right, left, to_right, to_left, cut_at):
-        a, b = pl.ds(0, cut_at), pl.ds(cut_at, cut_at)
+        a, b = cut_at
         send[1] = make(right).astype(BF)
         rb = remote(send.at[1, b], fin.at[0, b], to_right)
         send[2] = make(left).astype(BF)
@@ -233,31 +286,28 @@
         return rb, la
 
     def scatter_relay(send, rin, fin, first, plain, to_right, to_left, cut_at):
-        a, b = pl.ds(0, cut_at), pl.ds(cut_at, cut_at)
+        a, b = cut_at
         ra, lb = first
         rb, la = plain
         ra.wait_recv()
-        send[1, a] = (send[1, a].astype(F32) + rin[0].astype(F32)).astype(BF)
+        send[1, a] = (send[1, a].astype(F32) + rin[a].astype(F32)).astype(BF)
         fa = remote(send.at[1, a], fin.at[0, a], to_right)
         lb.wait_recv()
-        send[2, b] = (send[2, b].astype(F32) + rin[1].astype(F32)).astype(BF)
+        send[2, b] = (send[2, b].astype(F32) + rin[b].astype(F32)).astype(BF)
         fb = remote(send.at[2, b], fin.at[1, b], to_left)
         return rb, la, fa, fb
 
+    cut_y = lo, hi
+
     def branch(u):
         return dot(wo_t[pl.ds(pl.multiple_of(u * COLS, COLS), COLS), :], att)
 
     b_send, b_rin, b_fin = rs_send.at[0], rs_rin.at[0], rs_fin.at[0]
-    b_far = scatter_far(b_send, b_rin, branch, t_far, y_right, y_left, half)
-
-    gather_finish(go_rest)
-    grad_att = dot(wout_ref[...], go_full[...].reshape(MODEL, SEQ))
-    gas = [grad_att[h * HD : (h + 1) * HD].astype(BF) for h in range(2)]
+
+    b_far = scatter_far(b_send, b_rin, branch, t_far, y_right, y_left, cut_y)
     gvs = [dot(gas[h], saved[h][8], 1, 1) for h in range(2)]
     gp_buf[2] = jnp.concatenate(gvs, axis=0).astype(BF)
     v_copy = remote(gp_buf.at[2], gp_mate.at[2], mate)
-    go_copy = pick(1)
-
     gqs, gks = [], []
     for h in range(2):
         q_hat, q_inv, k_hat, k_inv, q, k, v, weights, weights_low = saved[h]
@@ -270,21 +320,29 @@
     gp_buf[1] = jnp.concatenate(gks, axis=0).astype(BF)
     qk_copy = remote(gp_buf.at[pl.ds(0, 2)], gp_mate.at[pl.ds(0, 2)], mate)
 
-    def grad_vo(u):
-        first = dot(own_sel[0, u], gp_buf[2], 1, 1) + dot(mate_sel[0, u], gp_mate[2], 1, 1)
-        second = dot(own_sel[1, u], gp_buf[3], 1, 1) + dot(mate_sel[1, u], gp_mate[3], 1, 1)
+    def vo_of(n_own, n_mate, go_own, go_mate):
+        first = dot(n_own, gp_buf[2], 1, 1) + dot(n_mate, gp_mate[2], 1, 1)
+        second = dot(go_own, gp_buf[3], 1, 1) + dot(go_mate, gp_mate[3], 1, 1)
         return jnp.concatenate([first, second], axis=1)
 
-    def grad_qk(u):
+    def qk_of(n_own, n_mate):
         ours = gp_buf[0:2].reshape(2 * QW, SEQ)
         theirs = gp_mate[0:2].reshape(2 * QW, SEQ)
-        return dot(own_sel[0, u], ours, 1, 1) + dot(mate_sel[0, u], theirs, 1, 1)
-
-    cut_x = KEPT // 2
-    n_copy.wait_recv()
-    att_copy.wait_recv()
-    v_copy.wait_recv()
-    go_copy.wait_recv()
+        return dot(n_own, ours, 1, 1) + dot(n_mate, theirs, 1, 1)
+
+    def grad_vo(u):
+        return vo_of(own_sel[0, u], mate_sel[0, u], own_sel[1, u], mate_sel[1, u])
+
+    def grad_qk(u):
+        return qk_of(own_sel[0, u], mate_sel[0, u])
+
+    cut_x = pl.ds(0, KEPT // 2), pl.ds(KEPT // 2, KEPT // 2)
+    order = [x_far, x_right, x_left, xi]
+    for u in order:
+        pick_own(1, u)
+        pick_own(0, u)
+    for copy in n_copies + go_copies + [att_copy, v_copy]:
+        copy.wait_recv()
     v_send, v_rin, v_fin = xs_send.at[0], xs_rin.at[0], xs_fin.at[0]
     q_send, q_rin, q_fin = xs_send.at[1], xs_rin.at[1], xs_fin.at[1]
     v_far = scatter_far(v_send, v_rin, grad_vo, x_far, px_right, px_left, cut_x)
@@ -307,22 +365,28 @@
         return rstd * (share[u] - s1 - ((rows_of(u) - mean) * rstd) * s2)
 
     g_send, g_rin, g_fin = rs_send.at[1], rs_rin.at[1], rs_fin.at[1]
-    g_far = scatter_far(g_send, g_rin, back, t_far, y_right, y_left, half)
-    g_plain = scatter_plain(g_send, g_fin, back, t_right, t_left, y_right, y_left, half)
+    g_far = scatter_far(g_send, g_rin, back, t_far, y_right, y_left, cut_y)
+    g_plain = scatter_plain(g_send, g_fin, back, t_right, t_left, y_right, y_left, cut_y)
 
     qk_copy.wait_recv()
     q_far = scatter_far(q_send, q_rin, grad_qk, x_far, px_right, px_left, cut_x)
+    rest_q = qk_of(own_rest[0], mate_rest[0])
+    rest_v = vo_of(own_rest[0], mate_rest[0], own_rest[1], mate_rest[1])
+    for k in range(NZ):
+        at = slice(k * REST, (k + 1) * REST)
+        rz_send[k] = jnp.concatenate([rest_q[at], rest_v[at]], axis=0).astype(BF)
+    rz_copies = [remote(rz_send.at[pz], rz_recv.at[zi], dev) for pz, dev in z_peers]
     q_plain = scatter_plain(
         q_send, q_fin, grad_qk, x_right, x_left, px_right, px_left, cut_x
     )
     v_rest = scatter_relay(v_send, v_rin, v_fin, v_far, v_plain, px_right, px_left, cut_x)
-    g_rest = scatter_relay(g_send, g_rin, g_fin, g_far, g_plain, y_right, y_left, half)
+    g_rest = scatter_relay(g_send, g_rin, g_fin, g_far, g_plain, y_right, y_left, cut_y)
     q_rest = scatter_relay(q_send, q_rin, q_fin, q_far, q_plain, px_right, px_left, cut_x)
-    b_plain = scatter_plain(b_send, b_fin, branch, t_right, t_left, y_right, y_left, half)
-    b_rest = scatter_relay(b_send, b_rin, b_fin, b_far, b_plain, y_right, y_left, half)
+    b_plain = scatter_plain(b_send, b_fin, branch, t_right, t_left, y_right, y_left, cut_y)
+    b_rest = scatter_relay(b_send, b_rin, b_fin, b_far, b_plain, y_right, y_left, cut_y)
 
     mixed_own = x_full[t].astype(F32) + branch(t)
-    gx_own = gout_ref[...].astype(F32) + back(t)
+    gx_own = go_full[t].astype(F32) + back(t)
     v_own = grad_vo(xi)
     q_own = grad_qk(xi)
 
@@ -335,16 +399,34 @@
     back_next = remote(bsnd_next, bfrom_prev, dp_next)
     back_prev = remote(bsnd_prev, bfrom_next, dp_prev)
 
-    for copy in v_rest:
+    def along_z(rest, mine, fin, slot):
+        for copy in rest:
+            copy.wait_recv()
+        summed = mine + fin[0].astype(F32) + fin[1].astype(F32)
+        z_send[slot] = summed.astype(BF).reshape(NZ, XROWS, COLS)
+        return [remote(z_send.at[slot, pz], z_recv.at[slot, zi], dev) for pz, dev in z_peers]
+
+    vz_copies = along_z(v_rest, v_own, v_fin, 1)
+    qz_copies = along_z(q_rest, q_own, q_fin, 0)
+
+    rest = rz_send[zi].astype(F32)
+    for copy in rz_copies:
         copy.wait_recv()
-    v_sum = v_own + v_fin[0].astype(F32) + v_fin[1].astype(F32)
-    for copy in q_rest:
-        copy.wait_recv()
-    q_sum = q_own + q_fin[0].astype(F32) + q_fin[1].astype(F32)
-    for k in range(NZ):
-        at = slice(k * CORE_ROWS, (k + 1) * CORE_ROWS)
-        z_send[k] = jnp.concatenate([q_sum[at], v_sum[at]], axis=0).astype(BF)
-    z_copies = [remote(z_send.at[pz], z_recv.at[zi], dev) for pz, dev in z_peers]
+    for pz, _ in z_peers:
+        rest = rest + rz_recv[pz].astype(F32)
+    r, c = grid2(NX * XROWS, 2 * REST)
+    mask = c < 0
+    for k in range(NX):
+        at = r - k * XROWS
+        mask = mask | ((at >= 0) & (at < ZROWS) & (c == at + k * ZROWS))
+        at = at - 8
+        mask = mask | ((at >= 0) & (at < ZROWS) & (c == at + k * ZROWS + REST))
+    rest = dot(hot(mask), rest.astype(BF)).astype(BF)
+    rx_send[...] = rest.reshape(NX, XROWS, COLS)
+    rx_copies = [
+        remote(rx_send.at[px], rx_recv.at[xi], (px * 16 + inner, t))
+        for px in (x_far, x_right, x_left)
+    ]
 
     length = SEQ + upper - lower
     behind = jnp.maximum(-lower, 0)
@@ -366,16 +448,31 @@
         copy.wait_recv()
     mixed_ref[...] = (mixed_own + b_fin[0].astype(F32) + b_fin[1].astype(F32)).astype(BF)
 
-    total = z_send[zi].astype(F32)
-    for copy in z_copies:
+    last = rx_send[xi].astype(F32)
+    for copy in rx_copies:
         copy.wait_recv()
-    for pz, _ in z_peers:
-        total = total + z_recv[pz].astype(F32)
-    total = total * total_scale
-    gqkv_ref[0] = total[0:SHARE, 0:QW]
-    gqkv_ref[1] = total[0:SHARE, QW : 2 * QW]
-    gqkv_ref[2] = total[CORE_ROWS : CORE_ROWS + SHARE, 0:QW]
-    gwout_ref[...] = total[CORE_ROWS : CORE_ROWS + SHARE, QW : 2 * QW]
+    for px in (x_far, x_right, x_left):
+        last = last + rx_recv[px].astype(F32)
+    last = last * total_scale
+
+    def finish(copies, slot):
+        total = z_send[slot, zi].astype(F32)
+        for copy in copies:
+            copy.wait_recv()
+        for pz, _ in z_peers:
+            total = total + z_recv[slot, pz].astype(F32)
+        return total * total_scale
+
+    vo = finish(vz_copies, 1)
+    qk = finish(qz_copies, 0)
+    gqkv_ref[0, 0:XROWS] = qk[:, 0:QW]
+    gqkv_ref[0, XROWS:SHARE] = last[0:ZROWS, 0:QW]
+    gqkv_ref[1, 0:XROWS] = qk[:, QW : 2 * QW]
+    gqkv_ref[1, XROWS:SHARE] = last[0:ZROWS, QW : 2 * QW]
+    gqkv_ref[2, 0:XROWS] = vo[:, 0:QW]
+    gqkv_ref[2, XROWS:SHARE] = last[8 : 8 + ZROWS, 0:QW]
+    gwout_ref[0:XROWS] = vo[:, QW : 2 * QW]
+    gwout_ref[XROWS:SHARE] = last[8 : 8 + ZROWS, QW : 2 * QW]
 
     for copy in pending:
         copy.wait_send()
@@ -388,21 +485,25 @@
     e_out[...] = e[...]
 
 
-COPIES = 56
+COPIES = 88
 
 
 def body(patches, seg_ids, cut, w_qkv, w_out, grad_out):
     vmem = pl.BlockSpec(memory_space=pltpu.VMEM)
+    anym = pl.BlockSpec(memory_space=pl.ANY)
     smem = pl.BlockSpec(memory_space=pltpu.SMEM)
     halo = pltpu.VMEM((SPILL, COLS), BF)
     scratch = [
+        pltpu.VMEM((COLS, SRC), BF),
+        pltpu.VMEM((3 * QW, MODEL), BF),
+        pltpu.VMEM((QW, MODEL), BF),
         pltpu.VMEM((2, NT, COLS, SEQ), BF),
         pltpu.VMEM((NT, COLS, SEQ), BF),
         pltpu.VMEM((MODEL, 3 * QW), BF),
         pltpu.VMEM((MODEL, QW), BF),
         halo, halo, halo, halo, halo, halo, halo, halo,
         pltpu.VMEM((2, 3, COLS, SEQ), BF),
-        pltpu.VMEM((2, 2, COLS // 2, SEQ), BF),
+        pltpu.VMEM((2, COLS, SEQ), BF),
         pltpu.VMEM((2, 2, COLS, SEQ), BF),
         pltpu.VMEM((NT, COLS, SEQ), F32),
         pltpu.VMEM((4, QW, SEQ), BF),
@@ -410,13 +511,22 @@
         pltpu.VMEM((2, NX, KEPT, SEQ), BF),
         pltpu.VMEM((2, NX, KEPT, SEQ), BF),
         pltpu.VMEM((2, NX, KEPT, SEQ), BF),
+        pltpu.VMEM((2, NZ * REST, MODEL), BF),
+        pltpu.VMEM((2, NZ * REST, SEQ), BF),
+        pltpu.VMEM((2, NZ * REST, SEQ), BF),
+        pltpu.VMEM((2, NZ * REST, SEQ), BF),
         pltpu.VMEM((2, 3, KEPT, COLS), BF),
-        pltpu.VMEM((2, 2, KEPT // 2, COLS), BF),
+        pltpu.VMEM((2, KEPT, COLS), BF),
         pltpu.VMEM((2, 2, KEPT, COLS), BF),
-        pltpu.VMEM((NZ, 2 * CORE_ROWS, COLS), BF),
-        pltpu.VMEM((NZ, 2 * CORE_ROWS, COLS), BF),
+        pltpu.VMEM((2, NZ, XROWS, COLS), BF),
+        pltpu.VMEM((2, NZ, XROWS, COLS), BF),
+        pltpu.VMEM((NZ, 2 * REST, COLS), BF),
+        pltpu.VMEM((NZ, 2 * REST, COLS), BF),
+        pltpu.VMEM((NX, XROWS, COLS), BF),
+        pltpu.VMEM((NX, XROWS, COLS), BF),
         pltpu.SemaphoreType.DMA((COPIES,)),
         pltpu.SemaphoreType.DMA((COPIES,)),
+        pltpu.SemaphoreType.DMA((4,)),
     ]
     out_shape = (
         jax.ShapeDtypeStruct((COLS, SEQ), BF),
@@ -427,7 +537,7 @@
     results = pl.pallas_call(
         kernel,
         out_shape=out_shape,
-        in_specs=[smem, vmem, vmem, vmem, vmem, vmem],
+        in_specs=[smem, vmem, anym, anym, anym, anym],
         out_specs=(vmem, vmem, vmem, vmem),
         scratch_shapes=scratch,
         compiler_params=pltpu.CompilerParams(

time: 53.8 us -> 48.8 us (0.907)
  Pallas kernels: 53 us -> 47.5 us
    pallas_call x1, Pallas kernels: 51.2 us -> 45.7 us  [body(): pl.pallas_call(kernel, out_shape=out_shape, in_specs=[smem, vmem, anym, a...]
where the time goes in v5:
time: 48.8 us; the launch traced here: 48.2 us
  Pallas kernels  47.5 us (97%)
  between operations  0.64 us (1%)
    pallas_call x1, Pallas kernels, body(): pl.pallas_call(kernel, out_shape=out_shape, in_specs=[smem, vmem, anym, a...  45.7 us
    pallas_call x1, Pallas kernels, body(): pl.pallas_call(hand_out, out_shape=out_shape, in_specs=[vmem, vmem, vmem,...  1.86 us

profile of v5, /device:TPU:1, one launch (start us, length us, event | category | flops | bytes accessed | tf_op | source)
XLA Modules:
  0.0 48.2 jit_solution(9228546165613494333)
XLA Ops:
  0.6 45.7 %shard_map.93 = (bf16[352,256]{1,0:T(8,128)(2,1)}, bf16[352,384]{1,0:T(8,128)(2,1)}, f32[3,22,176]{2,1,0:T(8,128)}, f32[22,176]{1,0:T(8,128)}) custom-call(s32[1,2]{1,0:T(1,128)} %cut_ref.1, s32[1,256]{1,0:T(1,128)} %bitcast.11, bf16[352,384]{1,0:T(8,128)(2,1)} %bitcast.9, bf16[528,1408]{1,0:T(8,128)(2,1)} %bitcast.8, bf16[176,1408]{1,0:T(8,128)(2,1)} %wout_in.1, ...), custom_call_target="tpu_custom_call" | custom-call | tf_op jit(solution)/shard_map/pallas_call | solution.py:537
  46.3 1.9 %shard_map.94 = (bf16[352,256]{1,0:T(8,128)(2,1)}, bf16[352,384]{1,0:T(8,128)(2,1)}, f32[3,22,176]{2,1,0:T(8,128)}, f32[22,176]{1,0:T(8,128)}) custom-call(bf16[352,256]{1,0:T(8,128)(2,1)} %get-tuple-element.12.a, bf16[352,384]{1,0:T(8,128)(2,1)} %get-tuple-element.13.b, f32[3,22,176]{2,1,0:T(8,128)} %get-tuple-element.14.c, f32[22,176]{1,0:T(8,128)} %get-tuple-element.15.e), custom_call_target="tpu_custom_call" | custom-call | tf_op jit(solution)/shard_map/pallas_call | solution.py:547

commit v6 on v5

--- a/solution.py
+++ b/solution.py
@@ -46,11 +46,11 @@
 
 
 def kernel(
-    cut_ref, seg_ref, patches_in, wqkv_in, wout_in, gout_in,
-    mixed_ref, gpatch_ref, gqkv_ref, gwout_ref,
-    patches_ref, wqkv_ref, wout_ref, acts, x_full, w_t, wo_t,
+    cut_in, seg_in, patches_in, wqkv_in, wout_in, gout_in,
+    mixed_out, gpatch_out, gqkv_ref, gwout_ref,
+    cut_ref, seg_ref, mixed_ref, gpatch_ref, patches_ref, wqkv_ref, wout_ref, acts, x_full, w_t, wo_t,
     snd_next, snd_prev, from_prev, from_next, bsnd_next, bsnd_prev, bfrom_prev, bfrom_next,
-    rs_send, rs_rin, rs_fin, share, gp_buf, gp_mate, own_sel, out_sel, mate_sel,
+    rs_send, rs_rin, rs_fin, gp_buf, gp_mate, own_sel, out_sel, mate_sel,
     z_pick, own_rest, out_rest, mate_rest,
     xs_send, xs_rin, xs_fin, z_send, z_recv, rz_send, rz_recv, rx_send, rx_recv,
     ssem, rsem, lsem,
@@ -73,6 +73,13 @@
     ]
     n_low, go_full = acts.at[0], acts.at[1]
 
+    barrier = pltpu.get_barrier_semaphore()
+    px_far = (x_far * 16 + inner, t)
+    greet = [dp_next, dp_prev, y_right, y_left, px_right, px_left, px_far]
+    greet = greet + [p for _, p in z_peers]
+    for peer in greet:
+        pl.semaphore_signal(barrier, inc=1, device_id=peer, device_id_type=MESH)
+
     loads = [
         pltpu.make_async_copy(src, dst, lsem.at[k])
         for k, (src, dst) in enumerate(
@@ -81,18 +88,13 @@
                 (gout_in, go_full.at[t]),
                 (wqkv_in, wqkv_ref),
                 (wout_in, wout_ref),
+                (cut_in, cut_ref),
+                (seg_in, seg_ref),
             ]
         )
     ]
     for load in loads:
         load.start()
-
-    barrier = pltpu.get_barrier_semaphore()
-    px_far = (x_far * 16 + inner, t)
-    greet = [dp_next, dp_prev, y_right, y_left, px_right, px_left, px_far]
-    greet = greet + [p for _, p in z_peers]
-    for peer in greet:
-        pl.semaphore_signal(barrier, inc=1, device_id=peer, device_id_type=MESH)
 
     counter = [0]
     pending = []
@@ -108,6 +110,7 @@
         pending.append(copy)
         return copy
 
+    loads[4].wait()
     lower = cut_ref[0, 0]
     upper = cut_ref[0, 1]
     head = jnp.maximum(lower, 0)
@@ -127,8 +130,7 @@
     half = COLS // 2
     lo, hi = pl.ds(0, half), pl.ds(half, half)
 
-    lo_pieces = pl.ds(0, 96), pl.ds(96, 80)
-    hi_pieces = pl.ds(half, 96), pl.ds(half + 96, 80)
+    lo_pieces, hi_pieces = (lo,), (hi,)
 
     def gather_handed(full):
         handed = []
@@ -168,6 +170,7 @@
     loads[2].wait()
     loads[3].wait()
     w_t[...] = jnp.transpose(wqkv_ref[...])
+    w_sums = jnp.sum(wqkv_ref[...].astype(F32), axis=-1, keepdims=True)
     wo_t[...] = jnp.transpose(wout_ref[...])
 
     to_next.wait_recv()
@@ -182,29 +185,28 @@
     zk = sum((r >= k * XROWS).astype(jnp.int32) for k in range(1, NZ))
     at_x = r - zk * XROWS + 2 * SHARE * zk
     _, c = grid2(KEPT, COLS)
-    x_own, x_mate = (hot(c == at_x + SHARE * side) for side in (core, 1 - core))
+    x_pick = jnp.concatenate([hot(c == at_x + SHARE * side) for side in (core, 1 - core)], axis=0)
     r = lax.broadcasted_iota(jnp.int32, (NZ * REST, 1), 0)
     zk = sum((r >= k * REST).astype(jnp.int32) for k in range(1, NZ))
     r = r - zk * REST
     xk = sum((r >= k * ZROWS).astype(jnp.int32) for k in range(1, NX))
     at_z = r - xk * ZROWS + COLS * xk + 2 * SHARE * zk + XROWS
     _, c = grid2(NZ * REST, MODEL)
-    z_pick[0] = hot(c == at_z + SHARE * core)
-    z_pick[1] = hot(c == at_z + SHARE * (1 - core))
+    z_pick[0 : NZ * REST] = hot(c == at_z + SHARE * core)
+    z_pick[NZ * REST :] = hot(c == at_z + SHARE * (1 - core))
 
     def pick_rest(kind):
         everything = acts[kind].reshape(MODEL, SEQ)
-        out_rest[kind] = dot(z_pick[1], everything).astype(BF)
-        copy = remote(out_rest.at[kind], mate_rest.at[kind], mate)
-        own_rest[kind] = dot(z_pick[0], everything).astype(BF)
-        return copy
-
-    def pick(kind, u):
-        out_sel[kind, u] = dot(x_mate, acts[kind, u]).astype(BF)
-        return remote(out_sel.at[kind, u], mate_sel.at[kind, u], mate)
-
-    def pick_own(kind, u):
-        own_sel[kind, u] = dot(x_own, acts[kind, u]).astype(BF)
+        both = dot(z_pick[...], everything).astype(BF)
+        out_rest[kind] = both[NZ * REST :]
+        own_rest[kind] = both[0 : NZ * REST]
+        return remote(out_rest.at[kind], mate_rest.at[kind], mate)
+
+    def pick(kind, u, send=True):
+        both = dot(x_pick, acts[kind, u]).astype(BF)
+        out_sel[kind, u] = both[KEPT:]
+        own_sel[kind, u] = both[0:KEPT]
+        return remote(out_sel.at[kind, u], mate_sel.at[kind, u], mate) if send else None
 
     def rows_of(u):
         return x_full[u].astype(F32)
@@ -217,12 +219,13 @@
 
     x_rest = gather_relay(x_full, x_handed)
     gather_finish(go_other)
-    go_copies = [pick(1, u) for u in (t, t_left, t_right)]
+    for u in (t, t_left, t_right):
+        pick(1, u, False)
     gather_finish(x_other)
     stats = [chunk_stats(u) for u in (t, t_left, t_right)]
     gather_finish(go_rest)
-    go_copies.append(pick(1, t_far))
-    go_copies.append(pick_rest(1))
+    pick(1, t_far, False)
+    go_copies = [remote(out_sel.at[1], mate_sel.at[1], mate), pick_rest(1)]
     grad_att = dot(wout_ref[...], go_full[...].reshape(MODEL, SEQ))
     gas = [grad_att[h * HD : (h + 1) * HD].astype(BF) for h in range(2)]
     gather_finish(x_rest)
@@ -236,7 +239,9 @@
     for u in range(NT):
         n_low[u] = ((rows_of(u) - mean) * rstd).astype(BF)
     proj = dot(wqkv_ref[...], n_low[...].reshape(MODEL, SEQ))
-    n_copies = [pick(0, u) for u in range(NT)] + [pick_rest(0)]
+    for u in range(NT):
+        pick(0, u, False)
+    n_copies = [remote(out_sel.at[0], mate_sel.at[0], mate)]
 
     def head_norm(v):
         center = v - jnp.sum(v, axis=0, keepdims=True) * (1.0 / HD)
@@ -249,6 +254,7 @@
         second = jnp.sum(g * normed, axis=0, keepdims=True) * (1.0 / HD)
         return inverse * (g - first - normed * second)
 
+    loads[5].wait()
     seg_row = seg_ref[...].astype(F32)
     r, c = grid2(SEQ, SEQ)
     seg_col = jnp.sum(jnp.where(r == c, seg_row, 0.0), axis=-1, keepdims=True)
@@ -338,9 +344,7 @@
 
     cut_x = pl.ds(0, KEPT // 2), pl.ds(KEPT // 2, KEPT // 2)
     order = [x_far, x_right, x_left, xi]
-    for u in order:
-        pick_own(1, u)
-        pick_own(0, u)
+    rest_copy = pick_rest(0)
     for copy in n_copies + go_copies + [att_copy, v_copy]:
         copy.wait_recv()
     v_send, v_rin, v_fin = xs_send.at[0], xs_rin.at[0], xs_fin.at[0]
@@ -351,18 +355,13 @@
     )
 
     gp = gp_buf[0:3].reshape(3 * QW, SEQ)
-    s1 = jnp.zeros((1, SEQ), F32)
-    s2 = jnp.zeros((1, SEQ), F32)
-    for u in range(NT):
-        part = dot(w_t[u * COLS : (u + 1) * COLS, :], gp)
-        share[u] = part
-        s1 = s1 + jnp.sum(part, axis=0, keepdims=True)
-        s2 = s2 + jnp.sum(part * ((rows_of(u) - mean) * rstd), axis=0, keepdims=True)
-    s1 = s1 * (1.0 / MODEL)
-    s2 = s2 * (1.0 / MODEL)
+    gp_wide = gp.astype(F32)
+    s1 = jnp.sum(gp_wide * w_sums, axis=0, keepdims=True) * (1.0 / MODEL)
+    s2 = jnp.sum(gp_wide * proj, axis=0, keepdims=True) * (1.0 / MODEL)
 
     def back(u):
-        return rstd * (share[u] - s1 - ((rows_of(u) - mean) * rstd) * s2)
+        part = dot(w_t[pl.ds(pl.multiple_of(u * COLS, COLS), COLS), :], gp)
+        return rstd * (part - s1 - ((rows_of(u) - mean) * rstd) * s2)
 
     g_send, g_rin, g_fin = rs_send.at[1], rs_rin.at[1], rs_fin.at[1]
     g_far = scatter_far(g_send, g_rin, back, t_far, y_right, y_left, cut_y)
@@ -370,6 +369,7 @@
 
     qk_copy.wait_recv()
     q_far = scatter_far(q_send, q_rin, grad_qk, x_far, px_right, px_left, cut_x)
+    rest_copy.wait_recv()
     rest_q = qk_of(own_rest[0], mate_rest[0])
     rest_v = vo_of(own_rest[0], mate_rest[0], own_rest[1], mate_rest[1])
     for k in range(NZ):
@@ -406,6 +406,8 @@
         z_send[slot] = summed.astype(BF).reshape(NZ, XROWS, COLS)
         return [remote(z_send.at[slot, pz], z_recv.at[slot, zi], dev) for pz, dev in z_peers]
 
+    earlier = list(pending)
+    pending.clear()
     vz_copies = along_z(v_rest, v_own, v_fin, 1)
     qz_copies = along_z(q_rest, q_own, q_fin, 0)
 
@@ -443,10 +445,16 @@
         src_rows + dot(bfrom_prev[...], pick_prev, 0, 0) + dot(bfrom_next[...], pick_next, 0, 0)
     )
     gpatch_ref[...] = src_rows.astype(BF)
-
+    gpatch_copy = pltpu.make_async_copy(gpatch_ref, gpatch_out, lsem.at[6])
+    gpatch_copy.start()
+
+    for copy in earlier:
+        copy.wait_send()
     for copy in b_rest:
         copy.wait_recv()
     mixed_ref[...] = (mixed_own + b_fin[0].astype(F32) + b_fin[1].astype(F32)).astype(BF)
+    mixed_copy = pltpu.make_async_copy(mixed_ref, mixed_out, lsem.at[7])
+    mixed_copy.start()
 
     last = rx_send[xi].astype(F32)
     for copy in rx_copies:
@@ -476,6 +484,8 @@
 
     for copy in pending:
         copy.wait_send()
+    gpatch_copy.wait()
+    mixed_copy.wait()
 
 
 def hand_out(a, b, c, e, a_out, b_out, c_out, e_out):
@@ -491,9 +501,12 @@
 def body(patches, seg_ids, cut, w_qkv, w_out, grad_out):
     vmem = pl.BlockSpec(memory_space=pltpu.VMEM)
     anym = pl.BlockSpec(memory_space=pl.ANY)
-    smem = pl.BlockSpec(memory_space=pltpu.SMEM)
     halo = pltpu.VMEM((SPILL, COLS), BF)
     scratch = [
+        pltpu.SMEM((1, 2), jnp.int32),
+        pltpu.VMEM((1, SEQ), jnp.int32),
+        pltpu.VMEM((COLS, SEQ), BF),
+        pltpu.VMEM((COLS, SRC), BF),
         pltpu.VMEM((COLS, SRC), BF),
         pltpu.VMEM((3 * QW, MODEL), BF),
         pltpu.VMEM((QW, MODEL), BF),
@@ -505,13 +518,12 @@
         pltpu.VMEM((2, 3, COLS, SEQ), BF),
         pltpu.VMEM((2, COLS, SEQ), BF),
         pltpu.VMEM((2, 2, COLS, SEQ), BF),
-        pltpu.VMEM((NT, COLS, SEQ), F32),
         pltpu.VMEM((4, QW, SEQ), BF),
         pltpu.VMEM((4, QW, SEQ), BF),
         pltpu.VMEM((2, NX, KEPT, SEQ), BF),
         pltpu.VMEM((2, NX, KEPT, SEQ), BF),
         pltpu.VMEM((2, NX, KEPT, SEQ), BF),
-        pltpu.VMEM((2, NZ * REST, MODEL), BF),
+        pltpu.VMEM((2 * NZ * REST, MODEL), BF),
         pltpu.VMEM((2, NZ * REST, SEQ), BF),
         pltpu.VMEM((2, NZ * REST, SEQ), BF),
         pltpu.VMEM((2, NZ * REST, SEQ), BF),
@@ -526,7 +538,7 @@
         pltpu.VMEM((NX, XROWS, COLS), BF),
         pltpu.SemaphoreType.DMA((COPIES,)),
         pltpu.SemaphoreType.DMA((COPIES,)),
-        pltpu.SemaphoreType.DMA((4,)),
+        pltpu.SemaphoreType.DMA((8,)),
     ]
     out_shape = (
         jax.ShapeDtypeStruct((COLS, SEQ), BF),
@@ -537,8 +549,8 @@
     results = pl.pallas_call(
         kernel,
         out_shape=out_shape,
-        in_specs=[smem, vmem, anym, anym, anym, anym],
-        out_specs=(vmem, vmem, vmem, vmem),
+        in_specs=[anym, anym, anym, anym, anym, anym],
+        out_specs=(anym, anym, vmem, vmem),
         scratch_shapes=scratch,
         compiler_params=pltpu.CompilerParams(
             collective_id=0, has_side_effects=True, vmem_limit_bytes=56 * 1024 * 1024

time: 48.8 us -> 47.9 us (0.982)
  no operation moved by 1% of the time
where the time goes in v6:
time: 47.9 us; the launch traced here: 47.7 us
  Pallas kernels  47.1 us (98%)
  between operations  0.64 us (1%)
    pallas_call x1, Pallas kernels, body(): pl.pallas_call(kernel, out_shape=out_shape, in_specs=[anym, anym, anym, a...  45.2 us
    pallas_call x1, Pallas kernels, body(): pl.pallas_call(hand_out, out_shape=out_shape, in_specs=[vmem, vmem, vmem,...  1.86 us

profile of v6, /device:TPU:1, one launch (start us, length us, event | category | flops | bytes accessed | tf_op | source)
XLA Modules:
  0.0 47.7 jit_solution(11495729806391718061)
XLA Ops:
  0.6 45.2 %shard_map.93 = (bf16[352,256]{1,0:T(8,128)(2,1)}, bf16[352,384]{1,0:T(8,128)(2,1)}, f32[3,22,176]{2,1,0:T(8,128)}, f32[22,176]{1,0:T(8,128)}) custom-call(s32[1,2]{1,0:T(1,128)} %cut_in.1, s32[1,256]{1,0:T(1,128)} %bitcast.11, bf16[352,384]{1,0:T(8,128)(2,1)} %bitcast.9, bf16[528,1408]{1,0:T(8,128)(2,1)} %bitcast.8, bf16[176,1408]{1,0:T(8,128)(2,1)} %wout_in.1, ...), custom_call_target="tpu_custom_call" | custom-call | tf_op jit(solution)/shard_map/pallas_call | solution.py:549
  45.9 1.9 %shard_map.94 = (bf16[352,256]{1,0:T(8,128)(2,1)}, bf16[352,384]{1,0:T(8,128)(2,1)}, f32[3,22,176]{2,1,0:T(8,128)}, f32[22,176]{1,0:T(8,128)}) custom-call(bf16[352,256]{1,0:T(8,128)(2,1)} %get-tuple-element.12.a, bf16[352,384]{1,0:T(8,128)(2,1)} %get-tuple-element.13.b, f32[3,22,176]{2,1,0:T(8,128)} %get-tuple-element.14.c, f32[22,176]{1,0:T(8,128)} %get-tuple-element.15.e), custom_call_target="tpu_custom_call" | custom-call | tf_op jit(solution)/shard_map/pallas_call | solution.py:559

commit v7 on v6

--- a/solution.py
+++ b/solution.py
@@ -69,7 +69,7 @@
     y_right, y_left = (d, t_right), (d, t_left)
     px_right, px_left = (x_right * 16 + inner, t), (x_left * 16 + inner, t)
     z_peers = [
-        (lax.rem(zi + k, NZ), (xi * 16 + lax.rem(zi + k, NZ) * 2 + core, t)) for k in (4, 3, 5, 2, 6, 1, 7)
+        (lax.rem(zi + k, NZ), (xi * 16 + lax.rem(zi + k, NZ) * 2 + core, t)) for k in (4, 1, 3, 7, 5, 2, 6)
     ]
     n_low, go_full = acts.at[0], acts.at[1]
 
@@ -274,7 +274,6 @@
         saved.append((q_hat, q_inv, k_hat, k_inv, q, k, v, weights, weights_low))
     att = jnp.concatenate(att_parts, axis=0).astype(BF)
     gp_buf[3] = att
-    att_copy = remote(gp_buf.at[3], gp_mate.at[3], mate)
 
     def scatter_far(send, rin, make, far, to_right, to_left, cut_at):
         a, b = cut_at
@@ -313,7 +312,7 @@
     b_far = scatter_far(b_send, b_rin, branch, t_far, y_right, y_left, cut_y)
     gvs = [dot(gas[h], saved[h][8], 1, 1) for h in range(2)]
     gp_buf[2] = jnp.concatenate(gvs, axis=0).astype(BF)
-    v_copy = remote(gp_buf.at[2], gp_mate.at[2], mate)
+    v_copy = remote(gp_buf.at[pl.ds(2, 2)], gp_mate.at[pl.ds(2, 2)], mate)
     gqs, gks = [], []
     for h in range(2):
         q_hat, q_inv, k_hat, k_inv, q, k, v, weights, weights_low = saved[h]
@@ -345,7 +344,7 @@
     cut_x = pl.ds(0, KEPT // 2), pl.ds(KEPT // 2, KEPT // 2)
     order = [x_far, x_right, x_left, xi]
     rest_copy = pick_rest(0)
-    for copy in n_copies + go_copies + [att_copy, v_copy]:
+    for copy in n_copies + go_copies + [v_copy]:
         copy.wait_recv()
     v_send, v_rin, v_fin = xs_send.at[0], xs_rin.at[0], xs_fin.at[0]
     q_send, q_rin, q_fin = xs_send.at[1], xs_rin.at[1], xs_fin.at[1]
@@ -365,10 +364,7 @@
 
     g_send, g_rin, g_fin = rs_send.at[1], rs_rin.at[1], rs_fin.at[1]
     g_far = scatter_far(g_send, g_rin, back, t_far, y_right, y_left, cut_y)
-    g_plain = scatter_plain(g_send, g_fin, back, t_right, t_left, y_right, y_left, cut_y)
-
     qk_copy.wait_recv()
-    q_far = scatter_far(q_send, q_rin, grad_qk, x_far, px_right, px_left, cut_x)
     rest_copy.wait_recv()
     rest_q = qk_of(own_rest[0], mate_rest[0])
     rest_v = vo_of(own_rest[0], mate_rest[0], own_rest[1], mate_rest[1])
@@ -376,11 +372,14 @@
         at = slice(k * REST, (k + 1) * REST)
         rz_send[k] = jnp.concatenate([rest_q[at], rest_v[at]], axis=0).astype(BF)
     rz_copies = [remote(rz_send.at[pz], rz_recv.at[zi], dev) for pz, dev in z_peers]
+    g_plain = scatter_plain(g_send, g_fin, back, t_right, t_left, y_right, y_left, cut_y)
+
+    q_far = scatter_far(q_send, q_rin, grad_qk, x_far, px_right, px_left, cut_x)
     q_plain = scatter_plain(
         q_send, q_fin, grad_qk, x_right, x_left, px_right, px_left, cut_x
     )
+    g_rest = scatter_relay(g_send, g_rin, g_fin, g_far, g_plain, y_right, y_left, cut_y)
     v_rest = scatter_relay(v_send, v_rin, v_fin, v_far, v_plain, px_right, px_left, cut_x)
-    g_rest = scatter_relay(g_send, g_rin, g_fin, g_far, g_plain, y_right, y_left, cut_y)
     q_rest = scatter_relay(q_send, q_rin, q_fin, q_far, q_plain, px_right, px_left, cut_x)
     b_plain = scatter_plain(b_send, b_fin, branch, t_right, t_left, y_right, y_left, cut_y)
     b_rest = scatter_relay(b_send, b_rin, b_fin, b_far, b_plain, y_right, y_left, cut_y)

time: 47.9 us -> 47.3 us (0.987)
  Pallas kernels: 47.1 us -> 46.3 us
    pallas_call x1, Pallas kernels: 45.2 us -> 44.5 us  [body(): pl.pallas_call(kernel, out_shape=out_shape, in_specs=[anym, anym, anym, a...]
where the time goes in v7:
time: 47.3 us; the launch traced here: 47 us
  Pallas kernels  46.3 us (98%)
  between operations  0.64 us (1%)
    pallas_call x1, Pallas kernels, body(): pl.pallas_call(kernel, out_shape=out_shape, in_specs=[anym, anym, anym, a...  44.5 us
    pallas_call x1, Pallas kernels, body(): pl.pallas_call(hand_out, out_shape=out_shape, in_specs=[vmem, vmem, vmem,...  1.86 us

profile of v7, /device:TPU:1, one launch (start us, length us, event | category | flops | bytes accessed | tf_op | source)
XLA Modules:
  0.0 47.0 jit_solution(10181439252822458724)
XLA Ops:
  0.6 44.5 %shard_map.93 = (bf16[352,256]{1,0:T(8,128)(2,1)}, bf16[352,384]{1,0:T(8,128)(2,1)}, f32[3,22,176]{2,1,0:T(8,128)}, f32[22,176]{1,0:T(8,128)}) custom-call(s32[1,2]{1,0:T(1,128)} %cut_in.1, s32[1,256]{1,0:T(1,128)} %bitcast.11, bf16[352,384]{1,0:T(8,128)(2,1)} %bitcast.9, bf16[528,1408]{1,0:T(8,128)(2,1)} %bitcast.8, bf16[176,1408]{1,0:T(8,128)(2,1)} %wout_in.1, ...), custom_call_target="tpu_custom_call" | custom-call | tf_op jit(solution)/shard_map/pallas_call | solution.py:548
  45.1 1.9 %shard_map.94 = (bf16[352,256]{1,0:T(8,128)(2,1)}, bf16[352,384]{1,0:T(8,128)(2,1)}, f32[3,22,176]{2,1,0:T(8,128)}, f32[22,176]{1,0:T(8,128)}) custom-call(bf16[352,256]{1,0:T(8,128)(2,1)} %get-tuple-element.12.a, bf16[352,384]{1,0:T(8,128)(2,1)} %get-tuple-element.13.b, f32[3,22,176]{2,1,0:T(8,128)} %get-tuple-element.14.c, f32[22,176]{1,0:T(8,128)} %get-tuple-element.15.e), custom_call_target="tpu_custom_call" | custom-call | tf_op jit(solution)/shard_map/pallas_call | solution.py:558

commit v8 on v7

--- a/solution.py
+++ b/solution.py
@@ -130,11 +130,15 @@
     half = COLS // 2
     lo, hi = pl.ds(0, half), pl.ds(half, half)
 
-    lo_pieces, hi_pieces = (lo,), (hi,)
-
-    def gather_handed(full):
+    halves = [(lo, hi)]
+    pieces = [
+        (pl.ds(0, 96), pl.ds(half, 96)),
+        (pl.ds(96, 80), pl.ds(half + 96, 80)),
+    ]
+
+    def gather_handed(full, cuts):
         handed = []
-        for low, high in zip(lo_pieces, hi_pieces):
+        for low, high in cuts:
             handed.append(remote(full.at[t, low], full.at[t, low], y_right))
             handed.append(remote(full.at[t, high], full.at[t, high], y_left))
         return handed
@@ -144,9 +148,9 @@
         la = remote(full.at[t, lo], full.at[t, lo], y_left)
         return [rb, la]
 
-    def gather_relay(full, handed):
+    def gather_relay(full, handed, cuts):
         rest = []
-        for k, (low, high) in enumerate(zip(lo_pieces, hi_pieces)):
+        for k, (low, high) in enumerate(cuts):
             handed[2 * k].wait_recv()
             rest.append(remote(full.at[t_left, low], full.at[t_left, low], y_right))
             handed[2 * k + 1].wait_recv()
@@ -158,7 +162,7 @@
             copy.wait_recv()
 
     loads[1].wait()
-    go_handed = gather_handed(go_full)
+    go_handed = gather_handed(go_full, halves)
     go_other = gather_other(go_full)
 
     r, c = grid2(SRC, SEQ)
@@ -177,9 +181,9 @@
     to_prev.wait_recv()
     own = own + dot(from_prev[...], pick_prev, 0, 0) + dot(from_next[...], pick_next, 0, 0)
     x_full[t] = own.astype(BF)
-    x_handed = gather_handed(x_full)
+    x_handed = gather_handed(x_full, pieces)
     x_other = gather_other(x_full)
-    go_rest = gather_relay(go_full, go_handed)
+    go_rest = gather_relay(go_full, go_handed, halves)
 
     r = lax.broadcasted_iota(jnp.int32, (KEPT, 1), 0)
     zk = sum((r >= k * XROWS).astype(jnp.int32) for k in range(1, NZ))
@@ -217,7 +221,7 @@
         rows = rows - centre
         return centre, jnp.sum(rows * rows, axis=0, keepdims=True)
 
-    x_rest = gather_relay(x_full, x_handed)
+    x_rest = gather_relay(x_full, x_handed, pieces)
     gather_finish(go_other)
     for u in (t, t_left, t_right):
         pick(1, u, False)

time: 47.3 us -> 47.3 us (level)
  no operation moved by 1% of the time
where the time goes in v8:
time: 47.3 us; the launch traced here: 47 us
  Pallas kernels  46.3 us (98%)
  between operations  0.64 us (1%)
    pallas_call x1, Pallas kernels, body(): pl.pallas_call(kernel, out_shape=out_shape, in_specs=[anym, anym, anym, a...  44.5 us
    pallas_call x1, Pallas kernels, body(): pl.pallas_call(hand_out, out_shape=out_shape, in_specs=[vmem, vmem, vmem,...  1.86 us

profile of v8, /device:TPU:1, one launch (start us, length us, event | category | flops | bytes accessed | tf_op | source)
XLA Modules:
  0.0 47.0 jit_solution(6791193291224763652)
XLA Ops:
  0.6 44.5 %shard_map.93 = (bf16[352,256]{1,0:T(8,128)(2,1)}, bf16[352,384]{1,0:T(8,128)(2,1)}, f32[3,22,176]{2,1,0:T(8,128)}, f32[22,176]{1,0:T(8,128)}) custom-call(s32[1,2]{1,0:T(1,128)} %cut_in.1, s32[1,256]{1,0:T(1,128)} %bitcast.11, bf16[352,384]{1,0:T(8,128)(2,1)} %bitcast.9, bf16[528,1408]{1,0:T(8,128)(2,1)} %bitcast.8, bf16[176,1408]{1,0:T(8,128)(2,1)} %wout_in.1, ...), custom_call_target="tpu_custom_call" | custom-call | tf_op jit(solution)/shard_map/pallas_call | solution.py:552
  45.1 1.9 %shard_map.94 = (bf16[352,256]{1,0:T(8,128)(2,1)}, bf16[352,384]{1,0:T(8,128)(2,1)}, f32[3,22,176]{2,1,0:T(8,128)}, f32[22,176]{1,0:T(8,128)}) custom-call(bf16[352,256]{1,0:T(8,128)(2,1)} %get-tuple-element.12.a, bf16[352,384]{1,0:T(8,128)(2,1)} %get-tuple-element.13.b, f32[3,22,176]{2,1,0:T(8,128)} %get-tuple-element.14.c, f32[22,176]{1,0:T(8,128)} %get-tuple-element.15.e), custom_call_target="tpu_custom_call" | custom-call | tf_op jit(solution)/shard_map/pallas_call | solution.py:562

commit v9 on v7

--- a/solution.py
+++ b/solution.py
@@ -69,7 +69,7 @@
     y_right, y_left = (d, t_right), (d, t_left)
     px_right, px_left = (x_right * 16 + inner, t), (x_left * 16 + inner, t)
     z_peers = [
-        (lax.rem(zi + k, NZ), (xi * 16 + lax.rem(zi + k, NZ) * 2 + core, t)) for k in (4, 1, 3, 7, 5, 2, 6)
+        (lax.rem(zi + k, NZ), (xi * 16 + lax.rem(zi + k, NZ) * 2 + core, t)) for k in (4, 3, 5, 2, 6, 1, 7)
     ]
     n_low, go_full = acts.at[0], acts.at[1]
 

time: 47.3 us -> 47.1 us (level)
  no operation moved by 1% of the time
where the time goes in v9:
time: 47.1 us; the launch traced here: 47 us
  Pallas kernels  46.4 us (99%)
  between operations  0.64 us (1%)
    pallas_call x1, Pallas kernels, body(): pl.pallas_call(kernel, out_shape=out_shape, in_specs=[anym, anym, anym, a...  44.5 us
    pallas_call x1, Pallas kernels, body(): pl.pallas_call(hand_out, out_shape=out_shape, in_specs=[vmem, vmem, vmem,...  1.86 us

profile of v9, /device:TPU:1, one launch (start us, length us, event | category | flops | bytes accessed | tf_op | source)
XLA Modules:
  0.0 47.0 jit_solution(1622938445006777938)
XLA Ops:
  0.6 44.5 %shard_map.93 = (bf16[352,256]{1,0:T(8,128)(2,1)}, bf16[352,384]{1,0:T(8,128)(2,1)}, f32[3,22,176]{2,1,0:T(8,128)}, f32[22,176]{1,0:T(8,128)}) custom-call(s32[1,2]{1,0:T(1,128)} %cut_in.1, s32[1,256]{1,0:T(1,128)} %bitcast.11, bf16[352,384]{1,0:T(8,128)(2,1)} %bitcast.9, bf16[528,1408]{1,0:T(8,128)(2,1)} %bitcast.8, bf16[176,1408]{1,0:T(8,128)(2,1)} %wout_in.1, ...), custom_call_target="tpu_custom_call" | custom-call | tf_op jit(solution)/shard_map/pallas_call | solution.py:548
  45.2 1.9 %shard_map.94 = (bf16[352,256]{1,0:T(8,128)(2,1)}, bf16[352,384]{1,0:T(8,128)(2,1)}, f32[3,22,176]{2,1,0:T(8,128)}, f32[22,176]{1,0:T(8,128)}) custom-call(bf16[352,256]{1,0:T(8,128)(2,1)} %get-tuple-element.12.a, bf16[352,384]{1,0:T(8,128)(2,1)} %get-tuple-element.13.b, f32[3,22,176]{2,1,0:T(8,128)} %get-tuple-element.14.c, f32[22,176]{1,0:T(8,128)} %get-tuple-element.15.e), custom_call_target="tpu_custom_call" | custom-call | tf_op jit(solution)/shard_map/pallas_call | solution.py:558
